TPU v7x, 32 devices: a whole 2x2x4 slice. The times are simulated.
32 devices in a mesh: leaf: 8 (over z, core), gen: 4 (over y, x).
Axes of the slice: x: 2, y: 2, z: 4, core: 2. Of those that a mesh axis runs over, the one named last changes fastest.
Arguments:
- points: float32 [16, 8, 2, 512], P(None, 'leaf'), may hold values from 0 to 1
- generators: bfloat16 [16, 8, 2, 512, 128], P(None, 'leaf', None, 'gen'), may hold values from -6 to 6
- leaf_ranks: int32 [16, 8], P(None, 'leaf'), may hold values from 112 to 128
- translations: bfloat16 [16, 8, 128, 256], P(None, 'leaf'), may hold values from -0.5 to 0.5
- parent_ranks: int32 [8, 8], P(None, 'leaf'), may hold values from 128 to 160
Outputs:
- leaf_basis: float32 [16, 8, 2, 512, 128], P(None, 'leaf', None, 'gen')
- leaf_block: float32 [16, 8, 128, 128], P(None, 'leaf', 'gen')
- parent_basis: float32 [8, 8, 256, 256], P(None, 'leaf', 'gen')
- parent_block: float32 [8, 8, 256, 256], P(None, 'leaf', 'gen')
Inputs may be any that keep to these rules, and one draw needn't show every extreme that they name: `leaf_ranks`: a leaf's rank; generator columns from the rank on are ignored. `parent_ranks`: a parent's rank; translation columns from the rank on are ignored.
All inputs are finite; a program needn't handle non-finite values.
Results may differ from a plain program's by a relative error of at most 0.0003.
Values may be sent and summed in bfloat16 or wider, within the bound.
A program may use at most 128 MiB of HBM per device.

v0:
```python
import jax
import jax.numpy as jnp
from jax import lax
from jax.sharding import PartitionSpec as P

HIGHEST = lax.Precision.HIGHEST
RANGE_SCALE = 4.0
SIGMA_ONE = 1.0
SIGMA_TWO = 0.8
CROSS_CORR = 0.5
NUGGET = 0.1


def swapped(array, axis, apart):
    return lax.ppermute(array, axis, [(i, i ^ 1 << apart) for i in range(lax.axis_size(axis))])


def matern(first, second):
    across = first[..., 0, :, None] - second[..., 0, None, :]
    upward = first[..., 1, :, None] - second[..., 1, None, :]
    scaled = RANGE_SCALE * jnp.sqrt(across * across + upward * upward)
    decays = jnp.exp(-scaled)
    marginal_one = SIGMA_ONE * SIGMA_ONE * decays
    middle = CROSS_CORR * SIGMA_ONE * SIGMA_TWO * (1.0 + scaled) * decays
    smooth = SIGMA_TWO * SIGMA_TWO * (1.0 + scaled + scaled * scaled / 3.0) * decays
    top_row = jnp.stack([marginal_one, middle], -2)
    bottom_row = jnp.stack([middle, smooth], -2)
    return jnp.stack([top_row, bottom_row], -4)


def kernel_apply(near_coords, far_coords, far_columns):
    return jnp.einsum(
        "vnwp,wpk->vnk", matern(near_coords, far_coords), far_columns, precision=HIGHEST
    )


def one_product(member):
    near_coords, far_coords, far_columns = member
    return kernel_apply(near_coords, far_coords, far_columns.astype(jnp.float32))


def lower_inverse(matrix):
    factor_low = jnp.linalg.cholesky(matrix)
    identity = jnp.broadcast_to(jnp.eye(matrix.shape[-1], dtype=jnp.float32), matrix.shape)
    return (factor_low, jax.scipy.linalg.solve_triangular(factor_low, identity, lower=True))


def per_device(points, generators, leaf_ranks, translations, parent_ranks):
    leaf_count = generators.shape[0]
    half_count = leaf_count // 2
    row_share = generators.shape[3]
    rank_width = generators.shape[-1]
    parent_width = translations.shape[-1]
    gen_count = lax.axis_size("gen")
    gen_spot = lax.axis_index("gen")
    parity = lax.axis_index("leaf") % 2
    keep_start = parity * half_count
    give_start = (1 - parity) * half_count

    def select_half(values, offset):
        return lax.dynamic_slice_in_dim(values, offset, half_count, 0)

    coords = points[:, 0]
    column_keep = (lax.iota(jnp.int32, rank_width)[None, :] < leaf_ranks[:, 0][:, None]).astype(
        jnp.float32
    )
    masked = generators[:, 0] * column_keep[:, None, None, :].astype(jnp.bfloat16)
    mapped = translations[:, 0] * column_keep[:, :, None].astype(jnp.bfloat16)
    far_coords = swapped(coords, "leaf", 0)
    own_far_coords = select_half(far_coords, keep_start)
    local_gram = jnp.einsum("lvnk,lvnj->lkj", masked, masked, preferred_element_type=jnp.float32)
    gram_sum = lax.psum(local_gram, "gen") + jax.vmap(jnp.diag)(1.0 - column_keep)
    lows, inverses = lower_inverse(gram_sum)
    bases = jnp.einsum(
        "lvnk,ljk->lvnj", masked, inverses, precision=HIGHEST, preferred_element_type=jnp.float32
    )
    far_shards, far_maps = swapped(
        (select_half(masked, give_start), select_half(mapped, give_start)), "leaf", 0
    )
    local_rows = lax.dynamic_slice_in_dim(coords, gen_spot * row_share, row_share, 2)
    own_rows = select_half(local_rows, keep_start)
    piece_own = lax.all_gather(masked, "gen", axis=2, tiled=True)
    piece_far = lax.all_gather(far_shards, "gen", axis=2, tiled=True)
    nearby = lax.map(one_product, (local_rows, coords, piece_own))
    across = lax.map(one_product, (own_rows, own_far_coords, piece_far))
    projected = jnp.einsum("lvnk,lvnj->lkj", bases, nearby, precision=HIGHEST)
    local_blocks = jnp.einsum("lkj,lij->lki", projected, inverses, precision=HIGHEST)
    local_blocks = local_blocks + NUGGET * jnp.einsum(
        "lvnk,lvnj->lkj", bases, bases, precision=HIGHEST
    )
    local_raw = jnp.einsum(
        "lvnk,lvnj->lkj", select_half(bases, keep_start), across, precision=HIGHEST
    )
    blocks, raw = lax.psum((local_blocks, local_raw), "gen")
    far_block, far_low = swapped(
        (select_half(blocks, give_start), select_half(lows, give_start)), "leaf", 0
    )
    far_identity = jnp.broadcast_to(jnp.eye(rank_width, dtype=jnp.float32), far_low.shape)
    far_inverse = jax.scipy.linalg.solve_triangular(far_low, far_identity, lower=True)
    coupled = jnp.einsum("lkj,lij->lki", raw, far_inverse, precision=HIGHEST)
    own_block = select_half(blocks, keep_start)
    own_low = select_half(lows, keep_start)
    own_factor = jnp.einsum(
        "lkj,lkp->ljp",
        own_low,
        select_half(mapped, keep_start).astype(jnp.float32),
        precision=HIGHEST,
    )
    far_factor = jnp.einsum(
        "lkj,lkp->ljp", far_low, far_maps.astype(jnp.float32), precision=HIGHEST
    )
    is_even = parity == 0
    even_block = jnp.where(is_even, own_block, far_block)
    odd_block = jnp.where(is_even, far_block, own_block)
    even_factor = jnp.where(is_even, own_factor, far_factor)
    odd_factor = jnp.where(is_even, far_factor, own_factor)
    coupled = jnp.where(is_even, coupled, jnp.swapaxes(coupled, 1, 2))
    parent_keep = (lax.iota(jnp.int32, parent_width)[None, :] < parent_ranks[:, 0][:, None]).astype(
        jnp.float32
    )
    stacked = jnp.concatenate([even_factor, odd_factor], 1) * parent_keep[:, None, :]
    parent_gram = jnp.einsum("lak,laj->lkj", stacked, stacked, precision=HIGHEST) + jax.vmap(
        jnp.diag
    )(1.0 - parent_keep)
    parent_low, parent_inverse = lower_inverse(parent_gram)
    parent_bases = jnp.einsum("lak,ljk->laj", stacked, parent_inverse, precision=HIGHEST)
    top_row = jnp.concatenate([even_block, coupled], 2)
    bottom_row = jnp.concatenate([jnp.swapaxes(coupled, 1, 2), odd_block], 2)
    parent_matrix = jnp.concatenate([top_row, bottom_row], 1)
    mixed = jnp.einsum("lab,lbj->laj", parent_matrix, parent_bases, precision=HIGHEST)
    parent_blocks = jnp.einsum("lak,laj->lkj", parent_bases, mixed, precision=HIGHEST)
    leaf_share = rank_width // gen_count
    basis_share = 2 * rank_width // gen_count
    parent_share = parent_width // gen_count
    leaf_out = lax.dynamic_slice_in_dim(blocks, gen_spot * leaf_share, leaf_share, 1)
    basis_out = lax.dynamic_slice_in_dim(parent_bases, gen_spot * basis_share, basis_share, 1)
    block_out = lax.dynamic_slice_in_dim(parent_blocks, gen_spot * parent_share, parent_share, 1)
    return (bases[:, None], leaf_out[:, None], basis_out[:, None], block_out[:, None])


def solution(mesh):
    return jax.shard_map(
        per_device,
        mesh=mesh,
        in_specs=(
            P(None, "leaf", None, None),
            P(None, "leaf", None, "gen", None),
            P(None, "leaf"),
            P(None, "leaf", None, None),
            P(None, "leaf"),
        ),
        out_specs=(
            P(None, "leaf", None, "gen", None),
            P(None, "leaf", "gen", None),
            P(None, "leaf", "gen", None),
            P(None, "leaf", "gen", None),
        ),
        check_vma=False,
    )
```

profile of v0, /device:TPU:0, one launch (start us, length us, event | category | flops | bytes accessed | tf_op | source)
XLA Modules:
  0.0 1115.4 jit_solution(18055530516305526337)
XLA Ops:
  22.6 44.4 %all-reduce.5.cloned.1.call-done = f32[16,128,128]{2,1,0:T(8,128)} async-done(((f32[16,128,128]{2,1,0:T(8,128)}), f32[16,128,128]{2,1,0:T(8,128)}) %all-reduce.5.cloned.1.call-update) | async-done | bytes 1048592 | tf_op jit(solution)/shard_map/psum | solution.py:72
  70.0 187.5 %custom-call.29 = f32[16,128,128]{2,1,0:T(8,128)S(1)} custom-call(f32[16,128,128]{2,1,0:T(8,128)S(1)} %fusion.38), custom_call_target="Cholesky" | custom-call | tf_op jit(solution)/shard_map/jit(cholesky)/cholesky | solution.py:43
  259.6 158.3 %custom-call.30 = f32[16,1,128,128]{2,3,1,0:T(8,128)S(1)} custom-call(f32[16,1,128,128]{3,2,1,0:T(8,128)} %get-tuple-element.108), custom_call_target="InvertDiagBlocksLowerTriangular" | custom-call | tf_op jit(solution)/shard_map/jit(_solve_triangular)/vmap()/triangular_solve | solution.py:45
  422.5 4.5 fusion.33
  430.0 4.9 fusion.32
  434.9 3.3 copy.33
  438.2 2.7 fusion.31
  443.1 95.2 %custom-call.31 = f32[8,128,128]{2,1,0:T(8,128)} custom-call(f32[8,128,128]{2,1,0:T(8,128)} %cholesky.142), custom_call_target="Cholesky" | custom-call | tf_op jit(solution)/shard_map/jit(cholesky)/cholesky | solution.py:43
  538.3 2.7 cholesky.138
  542.1 80.0 %custom-call.32 = f32[8,1,128,128]{2,3,1,0:T(8,128)} custom-call(f32[8,1,128,128]{3,2,1,0:T(8,128)} %get-tuple-element.140), custom_call_target="InvertDiagBlocksLowerTriangular" | custom-call | tf_op jit(solution)/shard_map/jit(cholesky)/cholesky | solution.py:43
  622.1 2.7 constant_dynamic-update-slice_fusion.1
  624.8 3.1 convolution_subtract_fusion.1
  627.9 95.4 %custom-call.33 = f32[8,128,128]{2,1,0:T(8,128)} custom-call(f32[8,128,128]{2,1,0:T(8,128)} %convolution_subtract_fusion.1), custom_call_target="Cholesky" | custom-call | tf_op jit(solution)/shard_map/jit(cholesky)/cholesky | solution.py:43
  725.7 3.2 select_select_fusion
  728.9 32.4 %while.22 = (s32[]{:T(128)}, f32[8,2,128,128]{3,2,1,0:T(8,128)}, f32[8,2,128]{2,1,0:T(2,128)}, f32[8,2,512]{2,1,0:T(2,128)}, bf16[8,2,512,128]{3,2,1,0:T(8,128)(2,1)}, /*index=5*/s32[]{:T(128)}, s32[]{:T(128)}, s32[]{}) while((s32[]{:T(128)}, f32[8,2,128,128]{3,2,1,0:T(8,128)}, f32[8,2,128]{2,1,0:T(2,128)}, f32[8,2,512]{2,1,0:T(2,128)}, ...), condition=%wide.region_11.12_spmd, body=%wide.region_10.11_spmd.sunk | while | flops 404160512 | bytes 4081781 | solution.py:85
  761.3 3.9 convolution_bitcast_fusion.5
  765.2 65.0 %while.21 = (s32[]{:T(128)}, f32[16,2,128,128]{3,2,1,0:T(8,128)}, f32[16,2,128]{2,1,0:T(2,128)}, f32[16,2,512]{2,1,0:T(2,128)}, bf16[16,2,512,128]{3,2,1,0:T(8,128)(2,1)}, /*index=5*/s32[]{:T(128)}, s32[]{:T(128)}, s32[]{}) while((s32[]{:T(128)}, f32[16,2,128,128]{3,2,1,0:T(8,128)}, f32[16,2,128]{2,1,0:T(2,128)}, f32[16,2,512]{2,1,0:T(2,128)}, ...), condition=%wide.region_4.5_spmd, body=%wide.region_3.4_spmd.sunk | while | flops 404160512 | bytes 4081781 | solution.py:84
  830.2 5.3 convolution_bitcast_fusion.3
  835.6 3.3 convolution_add_fusion
  839.1 5.8 while.23
  842.5 2.3 bitcast_dynamic-update-slice_fusion.2
  844.8 158.6 %custom-call.34 = f32[8,2,128,128]{2,3,1,0:T(8,128)} custom-call(f32[8,2,128,128]{3,2,1,0:T(8,128)} %bitcast.188), custom_call_target="InvertDiagBlocksLowerTriangular" | custom-call | tf_op jit(solution)/shard_map/jit(_solve_triangular)/vmap()/triangular_solve | solution.py:45
  1003.5 80.3 %custom-call.35 = f32[8,1,128,128]{2,3,1,0:T(8,128)} custom-call(f32[8,1,128,128]{3,2,1,0:T(8,128)} %get-tuple-element.139), custom_call_target="InvertDiagBlocksLowerTriangular" | custom-call | tf_op jit(solution)/shard_map/jit(_solve_triangular)/vmap()/triangular_solve | solution.py:99
  1104.1 3.5 fusion.67
  (287 shorter events, 154.7 us)
Async XLA Ops:
  7.2 59.8 %all-reduce.5.cloned.1.call-start = ((), (), s32[]{:S(2)}) async-start(), calls=%async_computation | async-start | bytes 2097152 | tf_op jit(solution)/shard_map/psum | solution.py:72
  10.7 3.8 copy-start.27
  10.7 4.3 copy-start.20
  10.7 718.1 %all-gather.5.cloned.1.call-start = ((), (), s32[]{:S(2)}) async-start(), calls=%async_computation.2 | async-start | bytes 2621440 | tf_op jit(solution)/shard_map/all_gather | solution.py:83
  10.9 2.1 collective-permute-start.4
  13.7 4.2 copy-start.28
  13.7 4.3 copy-start.29
  13.8 751.4 %all-gather.3.cloned.1.call-start = ((), (), s32[]{:S(2)}) async-start(), calls=%async_computation.1 | async-start | bytes 5242880 | tf_op jit(solution)/shard_map/all_gather | solution.py:82
  14.5 1077.7 %all-reduce.7.cloned.1.call-start = ((), (), s32[]{:S(2)}) async-start(), calls=%async_computation.3 | async-start | bytes 3145728 | tf_op jit(solution)/shard_map/psum | solution.py:94
  14.6 7.4 collective-permute-start.3
  17.2 409.9 %collective-permute-start.1 = (bf16[8,128,256]{2,1,0:T(8,128)(2,1)}, bf16[8,128,256]{2,1,0:T(8,128)(2,1)}, u32[]{:S(2)}, u32[]{:S(2)}) collective-permute-start(bf16[8,128,256]{2,1,0:T(8,128)(2,1)} %constant_dynamic-slice_fusion.10), channel_id=1, source_target_pairs={{0,4},{4,0},{8,12},{12,8},{16,20},{20,16},{24,28},{28,24},{1,5},{5... | collective-permute-start | bytes 1572872 | tf_op jit(solution)/shard_map/ppermute | solution.py:15
  18.0 48.9 %copy-start.26 = (f32[16,128]{1,0:T(8,128)}, f32[16,128]{1,0:T(8,128)S(1)}, u32[]{:S(2)}) copy-start(f32[16,128]{1,0:T(8,128)S(1)} %convert_subtract_fusion) | copy-start | bytes 24580
  259.6 158.5 %copy-start.14 = (f32[16,128,128]{2,1,0:T(8,128)}, f32[16,128,128]{2,1,0:T(8,128)S(1)}, u32[]{:S(2)}) copy-start(f32[16,128,128]{2,1,0:T(8,128)S(1)} %get-tuple-element.109) | copy-start | bytes 3145732
  259.6 160.3 %copy-start.2 = (bf16[16,2,128,128]{3,2,1,0:T(8,128)(2,1)S(1)}, bf16[16,2,128,128]{3,2,1,0:T(8,128)(2,1)}, u32[]{:S(2)}) copy-start(bf16[16,2,128,128]{3,2,1,0:T(8,128)(2,1)} %copy-done.1) | copy-start | bytes 3145732
  418.0 9.0 collective-permute-start
  421.9 408.3 %copy-start = (f32[16,2,128,128]{3,2,1,0:T(8,128)}, f32[16,2,128,128]{3,2,1,0:T(8,128)S(1)}, u32[]{:S(2)}) copy-start(f32[16,2,128,128]{3,2,1,0:T(8,128)S(1)} %fusion.34) | copy-start | bytes 6291460
  427.0 2.9 copy-start.24
  830.2 5.4 copy-start.7
  830.2 5.4 copy-start.11
  835.6 3.4 copy-start.30
  835.6 3.5 copy-start.3
  1083.8 3.2 copy-start.19
  1088.1 3.1 copy-start.22
  1094.0 6.7 collective-permute-start.2
  (16 other events, 29.4 us)
Sparse Core Ops, SparseCore 0:
  11.6 55.2 all-reduce.4
  69.3 35.4 all-gather.4
  106.7 52.8 all-gather.2
  839.1 61.6 all-reduce.6
where the time goes:
time: 1130 us; the launch traced here: 1120 us
  other arithmetic  887 us (78%)
  matrix products  103 us (9%)
  local copies, waits for them, and re-layouts  61.7 us (5%)
  waiting for transfers between devices  46.7 us (4%)
  between operations  14.8 us (1%)
    another operation x11, other arithmetic, lower_inverse(): factor_low = jnp.linalg.cholesky(matrix)  461 us
    another operation x7, other arithmetic, lower_inverse(): jax.scipy.linalg.solve_triangular(factor_low, identity, lower=True)  323 us
    another operation x2, other arithmetic, per_device(): jax.scipy.linalg.solve_triangular(far_low, far_identity, lower=True)  81.3 us
    dot_general x24, matrix products, kernel_apply(): jnp.einsum('vnwp,wpk->vnk', matern(near_coords, far_coords), far_columns,...  53.1 us
    psum x1, waiting for transfers between devices, per_device(): lax.psum(local_gram, 'gen') + jax.vmap(jnp.diag)(1.0 - column_keep)  44.4 us
  transfers between devices with their start and end apart: 9, of which 2 were waited for; matrix products, arithmetic and copies ran while one was open for 86% of the time, Pallas kernels for 0%

commit v1 on v0

v1 whole, which is shorter than its diff:
```python
import functools

import jax
import jax.numpy as jnp
from jax import lax
from jax.experimental import pallas as pl
from jax.experimental.pallas import tpu as pltpu
from jax.sharding import PartitionSpec as P

HIGHEST = lax.Precision.HIGHEST
RANGE_SCALE = 4.0
SIGMA_ONE = 1.0
SIGMA_TWO = 0.8
CROSS_CORR = 0.5
NUGGET = 0.1
BLOCK = 32


def swapped(array):
    return lax.ppermute(array, "leaf", [(i, i ^ 1) for i in range(lax.axis_size("leaf"))])


def eliminate(steps, gram_ref, upper_ref, inverse_ref, work_ref):
    count, rows, width = gram_ref.shape
    lanes = lax.broadcasted_iota(jnp.int32, (1, width), 1)
    work_ref[...] = gram_ref[:, :steps, :]
    if steps < rows:
        upper_ref[:, steps:, :] = jnp.zeros((count, rows - steps, width), jnp.float32)
        inverse_ref[:, steps:, :] = jnp.zeros((count, rows - steps, width), jnp.float32)

    for start in range(0, steps, BLOCK):

        def step(k, carry, start=start):
            here = lanes == k
            for b in range(count):
                row = work_ref[b, pl.ds(k, 1), :]
                below = work_ref[b, start:, :]
                pivot = jnp.sum(jnp.where(here, row, 0.0), axis=1, keepdims=True)
                column = jnp.sum(jnp.where(here, below, 0.0), axis=1, keepdims=True)
                root = lax.rsqrt(pivot)
                root = root * (1.5 - 0.5 * pivot * root * root)
                upper_ref[b, pl.ds(k, 1), :] = jnp.where(lanes >= k, row, 0.0) * root
                one = jnp.where(here, 1.0, 0.0)
                inverse_ref[b, pl.ds(k, 1), :] = jnp.where(lanes < k, row, one) * root
                scaled = column * (root * root)
                work_ref[b, start:, :] = jnp.where(here, -scaled, below - scaled * row)
            return carry

        lax.fori_loop(start, start + BLOCK, step, 0)


def factor(gram, steps):
    shape = jax.ShapeDtypeStruct(gram.shape, jnp.float32)
    count, _, width = gram.shape
    return pl.pallas_call(
        functools.partial(eliminate, steps),
        out_shape=(shape, shape),
        scratch_shapes=[pltpu.VMEM((count, steps, width), jnp.float32)],
    )(gram)


def split(value):
    high = value.astype(jnp.bfloat16)
    return high, (value - high.astype(jnp.float32)).astype(jnp.bfloat16)


def times(value, exact):
    high, low = split(value)
    return jnp.dot(high, exact, preferred_element_type=jnp.float32) + jnp.dot(
        low, exact, preferred_element_type=jnp.float32
    )


def gather_covariance(near_ref, far_ref, near_rows_ref, far_rows_ref, out_ref):
    @pl.when(pl.program_id(1) == 0)
    def _():
        out_ref[...] = jnp.zeros_like(out_ref)

    near = near_ref[0]
    far = far_ref[0]
    across = near[:, 0:1] - far[0:1, :]
    upward = near[:, 1:2] - far[1:2, :]
    scaled = RANGE_SCALE * jnp.sqrt(across * across + upward * upward)
    decays = jnp.exp(-scaled)
    one = SIGMA_ONE * SIGMA_ONE * decays
    middle = (CROSS_CORR * SIGMA_ONE * SIGMA_TWO) * (1.0 + scaled) * decays
    smooth = (SIGMA_TWO * SIGMA_TWO) * (1.0 + scaled + scaled * scaled * (1.0 / 3.0)) * decays
    first, second = far_rows_ref[0, 0], far_rows_ref[0, 1]
    top = times(one, first) + times(middle, second)
    bottom = times(middle, first) + times(smooth, second)
    total = out_ref[0]
    for variable, image in ((0, top), (1, bottom)):
        for part in split(image):
            total = total + lax.dot_general(
                near_rows_ref[0, variable], part, (((0,), (0,)), ((), ())),
                preferred_element_type=jnp.float32,
            )
    out_ref[0] = total


def covariance(near_coords, far_coords, near_rows, far_rows):
    count, _, points, width = near_rows.shape
    tile = 128
    return pl.pallas_call(
        gather_covariance,
        grid=(count, points // tile),
        in_specs=[
            pl.BlockSpec((1, tile, 2), lambda i, j: (i, j, 0)),
            pl.BlockSpec((1, 2, points), lambda i, j: (i, 0, 0)),
            pl.BlockSpec((1, 2, tile, width), lambda i, j: (i, 0, j, 0)),
            pl.BlockSpec((1, 2, points, width), lambda i, j: (i, 0, 0, 0)),
        ],
        out_specs=pl.BlockSpec((1, width, width), lambda i, j: (i, 0, 0)),
        out_shape=jax.ShapeDtypeStruct((count, width, width), jnp.float32),
    )(jnp.swapaxes(near_coords, 1, 2), far_coords, near_rows, far_rows)


def sandwich(left, inner, right):
    mixed = jnp.einsum("lab,lcb->lac", inner, right, precision=HIGHEST)
    return jnp.einsum("lka,lac->lkc", left, mixed, precision=HIGHEST)


def per_device(points, generators, leaf_ranks, translations, parent_ranks):
    leaf_count, _, _, row_share, rank_width = generators.shape
    point_count = points.shape[-1]
    half = leaf_count // 2
    parent_width = translations.shape[-1]
    parent_most = parent_width * 5 // 8
    gens = lax.axis_size("gen")
    spot = lax.axis_index("gen")
    parity = lax.axis_index("leaf") % 2
    is_even = parity == 0
    sides = 2 if leaf_count // gens % 2 == 0 else 1
    each = leaf_count // (gens * sides)
    owned = sides * each

    def mine(values):
        values = values.reshape(sides, gens, each, *values.shape[1:])
        values = lax.dynamic_index_in_dim(values, spot, 1, keepdims=False)
        return values.reshape(owned, *values.shape[2:])

    def side(values, index):
        if sides == 1:
            return values
        return lax.dynamic_slice_in_dim(values, index * each, each, 0)

    local = generators[:, 0]
    spread = local.reshape(sides, gens, each, 2, row_share, rank_width)
    rows = lax.all_to_all(spread, "gen", split_axis=1, concat_axis=4, tiled=True)
    rows = rows.reshape(owned, 2, point_count, rank_width)
    coords = mine(points[:, 0])
    keep = (lax.iota(jnp.int32, rank_width)[None, :] < mine(leaf_ranks[:, 0])[:, None]).astype(
        jnp.float32
    )
    far_rows = swapped(side(rows, 1 - parity))
    far_coords = swapped(side(coords, 1 - parity))
    full = jnp.einsum("lvnk,lvnj->lkj", rows, rows, preferred_element_type=jnp.float32)
    eye = jnp.eye(rank_width, dtype=jnp.float32)
    gram = full * keep[:, :, None] * keep[:, None, :] + eye * (1.0 - keep)[:, None, :]
    upper, inverse = factor(gram, rank_width)
    upper = upper * keep[:, :, None]
    inverse = inverse * keep[:, :, None]
    every = lax.all_gather(inverse.reshape(sides, each, rank_width, rank_width), "gen", axis=1)
    every = every.reshape(leaf_count, rank_width, rank_width)

    factors = jnp.einsum(
        "lkj,ljp->lkp", upper, mine(translations[:, 0]).astype(jnp.float32), precision=HIGHEST
    )
    sums = covariance(
        jnp.concatenate([coords, side(coords, parity)], 0),
        jnp.concatenate([coords, far_coords], 0),
        jnp.concatenate([rows, side(rows, parity)], 0),
        jnp.concatenate([rows, far_rows], 0),
    )
    blocks = sandwich(inverse, sums[:owned] + NUGGET * full, inverse)
    bases = jnp.einsum(
        "lvnk,ljk->lvnj", local, every, precision=HIGHEST, preferred_element_type=jnp.float32
    )

    given = jnp.concatenate([factors, blocks, inverse], 2)
    far = swapped(side(given, 1 - parity))
    own_factor, own_block = side(factors, parity), side(blocks, parity)
    far_factor = far[:, :, :parent_width]
    far_block = far[:, :, parent_width : parent_width + rank_width]
    far_inverse = far[:, :, parent_width + rank_width :]
    coupled = sandwich(side(inverse, parity), sums[owned:], far_inverse)
    coupled = jnp.where(is_even, coupled, jnp.swapaxes(coupled, 1, 2))
    even_block = jnp.where(is_even, own_block, far_block)
    odd_block = jnp.where(is_even, far_block, own_block)
    even_factor = jnp.where(is_even, own_factor, far_factor)
    odd_factor = jnp.where(is_even, far_factor, own_factor)
    ranks = parent_ranks[:, 0]
    if sides == 1:
        other = swapped(ranks)
        ranks = jnp.where(
            is_even, jnp.concatenate([ranks, other]), jnp.concatenate([other, ranks])
        )
    ranks = lax.dynamic_slice_in_dim(ranks, spot * each, each, 0)
    parent_keep = (lax.iota(jnp.int32, parent_width)[None, :] < ranks[:, None]).astype(jnp.float32)
    stacked = jnp.concatenate([even_factor, odd_factor], 1) * parent_keep[:, None, :]
    parent_gram = jnp.einsum("lak,laj->lkj", stacked, stacked, precision=HIGHEST)
    parent_gram = parent_gram + jnp.eye(parent_width, dtype=jnp.float32) * (1.0 - parent_keep)[:, None, :]
    _, parent_inverse = factor(parent_gram, parent_most)
    parent_bases = jnp.einsum("lak,ljk->laj", stacked, parent_inverse, precision=HIGHEST)
    top_row = jnp.concatenate([even_block, coupled], 2)
    bottom_row = jnp.concatenate([jnp.swapaxes(coupled, 1, 2), odd_block], 2)
    parent_matrix = jnp.concatenate([top_row, bottom_row], 1)
    mixed = jnp.einsum("lab,lbj->laj", parent_matrix, parent_bases, precision=HIGHEST)
    parent_blocks = jnp.einsum("lak,laj->lkj", parent_bases, mixed, precision=HIGHEST)

    leaf_share = rank_width // gens
    basis_share = 2 * rank_width // gens
    parent_share = parent_width // gens
    lanes = 128
    tiles = parent_width // lanes

    def packed(values, share):
        values = values.reshape(each, gens, share, tiles, lanes)
        return values.transpose(1, 0, 3, 2, 4).reshape(gens, each * tiles * share, lanes)

    def unpacked(values, share):
        values = values.reshape(gens * each, tiles, share, lanes)
        if sides == 1:
            values = lax.dynamic_slice_in_dim(values, parity * half, half, 0)
        return values.transpose(0, 2, 1, 3).reshape(half, share, parent_width)

    leaf_pack = blocks.reshape(owned, gens, leaf_share, rank_width).transpose(1, 0, 2, 3)
    leaf_pack = leaf_pack.reshape(gens, owned * leaf_share, rank_width)
    pack = jnp.concatenate(
        [leaf_pack, packed(parent_bases, basis_share), packed(parent_blocks, parent_share)], 1
    )
    pack = lax.all_to_all(pack, "gen", split_axis=0, concat_axis=0, tiled=True)
    first = owned * leaf_share
    second = first + each * tiles * basis_share
    leaf_out = pack[:, :first].reshape(gens, sides, each, leaf_share, rank_width)
    leaf_out = leaf_out.transpose(1, 0, 2, 3, 4).reshape(leaf_count, leaf_share, rank_width)
    basis_out = unpacked(pack[:, first:second], basis_share)
    block_out = unpacked(pack[:, second:], parent_share)
    return (bases[:, None], leaf_out[:, None], basis_out[:, None], block_out[:, None])


def solution(mesh):
    return jax.shard_map(
        per_device,
        mesh=mesh,
        in_specs=(
            P(None, "leaf", None, None),
            P(None, "leaf", None, "gen", None),
            P(None, "leaf"),
            P(None, "leaf", None, None),
            P(None, "leaf"),
        ),
        out_specs=(
            P(None, "leaf", None, "gen", None),
            P(None, "leaf", "gen", None),
            P(None, "leaf", "gen", None),
            P(None, "leaf", "gen", None),
        ),
        check_vma=False,
    )
```

time: 1130 us -> 201 us (0.18); the launches traced: 1120 us -> 200 us
  other arithmetic: 887 us -> 10.2 us
  Pallas kernels: 0 us -> 112 us
  matrix products: 103 us -> 12.7 us
  local copies, waits for them, and re-layouts: 61.7 us -> 18.3 us
  waiting for transfers between devices: 46.7 us -> 21.9 us
    another operation x44 -> x0, other arithmetic: 868 us -> none  [the longest x11 461 us: lower_inverse(): factor_low = jnp.linalg.cholesky(matrix)]
    pallas_call x0 -> x3, Pallas kernels: none -> 112 us  [the longest x2 89.5 us: factor(): pl.pallas_call(functools.partial(eliminate, steps), out_shape=(shape, sha...]
    dot_general x33 -> x7, matrix products: 77.4 us -> 7.43 us  [the longest x2 2.01 us: sandwich(): mixed = jnp.einsum('lab,lcb->lac', inner, right, precision=HIGHEST)]
    psum x2 -> x0, waiting for transfers between devices: 44.4 us -> none  [the longest x1 44.4 us: per_device(): lax.psum(local_gram, 'gen') + jax.vmap(jnp.diag)(1.0 - column_keep)]
    all_to_all x0 -> x2, waiting for transfers between devices: none -> 20.4 us  [the longest x1 12.7 us: per_device(): pack = lax.all_to_all(pack, 'gen', split_axis=0, concat_axis=0, tiled=True)]
    dynamic_slice x31 -> x5, local copies, waits for them, and re-layouts: 20.5 us -> 2.34 us  [the longest x3 1.47 us: mine(): values = lax.dynamic_index_in_dim(values, spot, 1, keepdims=False)]
    slice x24 -> x2, local copies, waits for them, and re-layouts: 18.3 us -> 2.24 us  [the longest x1 1.27 us: per_device(): block_out = unpacked(pack[:, second:], parent_share)]
    another operation x7 -> x0, matrix products: 12.8 us -> none  [the longest x4 6.04 us: lower_inverse(): jax.scipy.linalg.solve_triangular(factor_low, identity, lower=True)]
  transfers between devices with their start and end apart: 9 -> 6, of which waited for: 2 -> 3; matrix products, arithmetic and copies ran while one was open for 86% -> 13% of each run, Pallas kernels for 0% -> 45%
where the time goes in v1:
time: 201 us; the launch traced here: 200 us
  Pallas kernels  112 us (56%)
  waiting for transfers between devices  21.9 us (11%)
  local copies, waits for them, and re-layouts  18.3 us (9%)
  between operations  14.3 us (7%)
  matrix products  12.7 us (6%)
  starting transfers between devices  10.3 us (5%)
  other arithmetic  10.2 us (5%)
    pallas_call x2, Pallas kernels, factor(): pl.pallas_call(functools.partial(eliminate, steps), out_shape=(shape, sha...  89.5 us
    pallas_call x1, Pallas kernels, covariance(): pl.pallas_call(gather_covariance, grid=(count, points // tile), in_specs=...  22.7 us
    all_to_all x1, waiting for transfers between devices, per_device(): pack = lax.all_to_all(pack, 'gen', split_axis=0, concat_axis=0, tiled=True)  12.7 us
    all_to_all x1, waiting for transfers between devices, per_device(): lax.all_to_all(spread, 'gen', split_axis=1, concat_axis=4, tiled=True)  7.62 us
    all_to_all x1, starting transfers between devices, per_device(): lax.all_to_all(spread, 'gen', split_axis=1, concat_axis=4, tiled=True)  5.29 us
    all_to_all x1, starting transfers between devices, per_device(): pack = lax.all_to_all(pack, 'gen', split_axis=0, concat_axis=0, tiled=True)  4.48 us
  transfers between devices with their start and end apart: 6, of which 3 were waited for; matrix products, arithmetic and copies ran while one was open for 13% of the time, Pallas kernels for 45%

profile of v1, /device:TPU:0, one launch (start us, length us, event | category | flops | bytes accessed | tf_op | source)
XLA Modules:
  0.0 199.9 jit_solution(9407877072169975128)
XLA Ops:
  7.2 2.4 %copy.68 = bf16[2,4,2,2,128,128]{5,4,3,2,0,1:T(8,128)(2,1)} copy(bf16[2,4,2,2,128,128]{5,4,3,2,1,0:T(8,128)(2,1)} %bitcast.80) | data formatting | bytes 2097152 | tf_op jit(solution)/shard_map/reshape;squeeze | solution.py:148
  9.6 5.3 %all-to-all-start = ((bf16[2,4,2,2,128,128]{5,4,3,2,0,1:T(8,128)(2,1)}), bf16[2,4,2,2,128,128]{5,4,3,2,0,1:T(8,128)(2,1)S(1)}, u32[]{:S(2)}, u32[]{:S(2)}) async-start(bf16[2,4,2,2,128,128]{5,4,3,2,0,1:T(8,128)(2,1)} %copy.68), calls=%async_computation | async-start | bytes 2097152 | tf_op jit(solution)/shard_map/all_to_all | solution.py:149
  19.2 1.7 copy.73.near_ref
  20.9 7.6 %all-to-all-done = bf16[2,4,2,2,128,128]{5,4,3,2,0,1:T(8,128)(2,1)S(1)} async-done(((bf16[2,4,2,2,128,128]{5,4,3,2,0,1:T(8,128)(2,1)}), bf16[2,4,2,2,128,128]{5,4,3,2,0,1:T(8,128)(2,1)S(1)}, u32[]{:S(2)}, u32[]{:S(2)}) %all-to-all-start) | async-done | bytes 1048608 | tf_op jit(solution)/shard_map/all_to_all | solution.py:149
  29.5 1.3 multiply_add_fusion
  30.8 52.6 %shard_map.84 = (f32[4,128,128]{2,1,0:T(8,128)}, f32[4,128,128]{2,1,0:T(8,128)}) custom-call(f32[4,128,128]{2,1,0:T(8,128)} %get-tuple-element.46.gram_ref), custom_call_target="tpu_custom_call" | custom-call | tf_op jit(solution)/shard_map/pallas_call | solution.py:55
  83.4 1.1 broadcast_multiply_fusion
  84.5 1.5 fusion.15
  86.0 2.9 %pad_maximum_fusion = (bf16[6,2,512,128]{3,2,1,0:T(8,128)(2,1)}, bf16[6,2,512,128]{3,2,1,0:T(8,128)(2,1)}) fusion(bf16[4,2,512,128]{3,2,1,0:T(8,128)(2,1)S(1)} %bitcast.77, bf16[2,2,512,128]{3,2,1,0:T(8,128)(2,1)} %collective-permute-done.1, bf16[2,2,512,128]{3,2,1,0:T(8,128)(2,1)S(1)} %get-tuple-element.37), kind=kLoop, calls=%fused_computation | loop fusion | flops 1572864 | bytes 5242880 | tf_op jit(solution)/shard_map/concatenate | solution.py:173
  88.9 22.7 %shard_map.85 = f32[6,128,128]{2,1,0:T(8,128)} custom-call(f32[6,512,2]{2,1,0:T(8,128)} %copy.73.near_ref, f32[6,2,512]{2,1,0:T(2,128)} %get-tuple-element.42.far_ref, bf16[6,2,512,128]{3,2,1,0:T(8,128)(2,1)} %get-tuple-element.35.near_rows_ref, bf16[6,2,512,128]{3,2,1,0:T(8,128)(2,1)} %get-tuple-element.34.far_rows_ref), custom_call_target="tpu_custom_call" | custom-call | tf_op jit(solution)/shard_map/pallas_call | solution.py:104
  111.6 1.6 fusion.12
  115.3 1.5 collective-permute-done.2
  117.2 1.2 fusion.21
  120.2 1.9 convolution_add_fusion.gram_ref
  122.0 36.9 %shard_map.86 = (f32[2,256,256]{2,1,0:T(8,128)}, f32[2,256,256]{2,1,0:T(8,128)}) custom-call(f32[2,256,256]{2,1,0:T(8,128)} %convolution_add_fusion.gram_ref), custom_call_target="tpu_custom_call" | custom-call | tf_op jit(solution)/shard_map/pallas_call | solution.py:55
  159.0 1.7 fusion.11
  164.0 1.2 pad_maximum_fusion.2
  165.2 4.5 %all-to-all-start.1 = ((f32[4,640,128]{2,1,0:T(8,128)}), f32[4,640,128]{2,1,0:T(8,128)}, u32[]{:S(2)}, u32[]{:S(2)}) async-start(f32[4,640,128]{2,1,0:T(8,128)} %pad_maximum_fusion.2), calls=%async_computation.1 | async-start | bytes 2621440 | tf_op jit(solution)/shard_map/all_to_all | solution.py:232
  169.7 1.4 copy.71
  172.3 1.8 copy.84
  174.1 12.7 %all-to-all-done.1 = f32[4,640,128]{2,1,0:T(8,128)} async-done(((f32[4,640,128]{2,1,0:T(8,128)}), f32[4,640,128]{2,1,0:T(8,128)}, u32[]{:S(2)}, u32[]{:S(2)}) %all-to-all-start.1) | async-done | bytes 1310752 | tf_op jit(solution)/shard_map/all_to_all | solution.py:232
  186.8 1.3 fusion.34
  188.5 1.2 broadcast_in_dim_reshape.11
  190.1 1.2 broadcast_in_dim_reshape.12
  (64 shorter events, 16.5 us)
Async XLA Ops:
  7.2 10.5 %copy-start = (bf16[16,1,128,256]{3,2,1,0:T(8,128)(2,1)S(1)}, bf16[16,1,128,256]{3,2,1,0:T(8,128)(2,1)}, u32[]{:S(2)}) copy-start(bf16[16,1,128,256]{3,2,1,0:T(8,128)(2,1)} %param.8) | copy-start | bytes 3145732
  9.6 7.3 %copy-start.8 = (s32[16,1]{0,1:T(1,128)S(1)}, s32[16,1]{0,1:T(1,128)}, u32[]{:S(2)}) copy-start(s32[16,1]{0,1:T(1,128)} %param.7) | copy-start | bytes 196
  9.6 18.9 %all-to-all-start = ((bf16[2,4,2,2,128,128]{5,4,3,2,0,1:T(8,128)(2,1)}), bf16[2,4,2,2,128,128]{5,4,3,2,0,1:T(8,128)(2,1)S(1)}, u32[]{:S(2)}, u32[]{:S(2)}) async-start(bf16[2,4,2,2,128,128]{5,4,3,2,0,1:T(8,128)(2,1)} %copy.68), calls=%async_computation | async-start | bytes 2097152 | tf_op jit(solution)/shard_map/all_to_all | solution.py:149
  14.9 154.8 %all-gather.2.cloned.1.call-start = ((), (), s32[]{:S(2)}) async-start(), calls=%async_computation.2 | async-start | bytes 1310720 | tf_op jit(solution)/shard_map/all_gather | solution.py:163
  15.6 3.0 %collective-permute-start = (f32[2,2,512]{2,1,0:T(2,128)S(1)}, f32[2,2,512]{2,1,0:T(2,128)S(1)}, u32[]{:S(2)}, u32[]{:S(2)}) collective-permute-start(f32[2,2,512]{2,1,0:T(2,128)S(1)} %get-tuple-element.44), channel_id=1, source_target_pairs={{0,4},{4,0},{8,12},{12,8},{16,20},{20,16},{24,28},{28,24},{1,5},{5... | collective-permute-start | bytes 24584 | tf_op jit(solution)/shard_map/ppermute | solution.py:20
  29.5 56.5 %collective-permute-start.1 = (bf16[2,2,512,128]{3,2,1,0:T(8,128)(2,1)}, bf16[2,2,512,128]{3,2,1,0:T(8,128)(2,1)}, u32[]{:S(2)}, u32[]{:S(2)}) collective-permute-start(bf16[2,2,512,128]{3,2,1,0:T(8,128)(2,1)} %get-tuple-element.36), channel_id=1, source_target_pairs={{0,4},{4,0},{8,12},{12,8},{16,20},{20,16},{24,28},{28,24},{1,5},{5... | collective-permute-start | bytes 1572872 | tf_op jit(solution)/shard_map/ppermute | solution.py:20
  84.5 29.2 %copy-start.1 = (f32[4,128,128]{2,1,0:T(8,128)}, f32[4,128,128]{2,1,0:T(8,128)S(1)}, u32[]{:S(2)}) copy-start(f32[4,128,128]{2,1,0:T(8,128)S(1)} %broadcast_multiply_fusion) | copy-start | bytes 786436
  88.9 22.7 %copy-start.5 = (f32[4,128,128]{2,1,0:T(8,128)S(1)}, f32[4,128,128]{2,1,0:T(8,128)}, u32[]{:S(2)}) copy-start(f32[4,128,128]{2,1,0:T(8,128)} %get-tuple-element.47) | copy-start | bytes 786436
  111.6 3.4 %copy-start.9 = (s32[8,1]{0,1:T(1,128)S(1)}, s32[8,1]{0,1:T(1,128)}, u32[]{:S(2)}) copy-start(s32[8,1]{0,1:T(1,128)} %param.9) | copy-start | bytes 100
  113.3 3.5 %copy-start.3 = (f32[6,128,128]{2,1,0:T(8,128)S(1)}, f32[6,128,128]{2,1,0:T(8,128)}, u32[]{:S(2)}) copy-start(f32[6,128,128]{2,1,0:T(8,128)} %shard_map.85) | copy-start | bytes 1179652
  114.5 5.6 %copy-start.4 = (f32[256,256]{1,0:T(8,128)S(1)}, f32[256,256]{1,0:T(8,128)}, u32[]{:S(2)}) copy-start(f32[256,256]{1,0:T(8,128)} %fusion.18) | copy-start | bytes 786436
  114.5 2.3 %collective-permute-start.2 = (f32[2,128,512]{2,1,0:T(8,128)}, f32[2,128,512]{2,1,0:T(8,128)S(1)}, u32[]{:S(2)}, u32[]{:S(2)}) collective-permute-start(f32[2,128,512]{2,1,0:T(8,128)} %fusion.2), channel_id=1, source_target_pairs={{0,4},{4,0},{8,12},{12,8},{16,20},{20,16},{24,28},{28,24},{1,5},{5... | collective-permute-start | bytes 1572872 | tf_op jit(solution)/shard_map/ppermute | solution.py:20
  116.8 1.6 copy-start.6
  122.0 38.9 %copy-start.7 = (f32[2,128,128]{1,2,0:T(8,128)S(1)}, f32[2,128,128]{1,2,0:T(8,128)}, u32[]{:S(2)}) copy-start(f32[2,128,128]{1,2,0:T(8,128)} %copy.78) | copy-start | bytes 393220
  165.2 21.6 %all-to-all-start.1 = ((f32[4,640,128]{2,1,0:T(8,128)}), f32[4,640,128]{2,1,0:T(8,128)}, u32[]{:S(2)}, u32[]{:S(2)}) async-start(f32[4,640,128]{2,1,0:T(8,128)} %pad_maximum_fusion.2), calls=%async_computation.1 | async-start | bytes 2621440 | tf_op jit(solution)/shard_map/all_to_all | solution.py:232
  169.7 1.5 copy-start.2
Sparse Core Ops, SparseCore 0:
  115.4 27.0 all-gather.1

commit v2 on v1

--- a/solution.py
+++ b/solution.py
@@ -14,6 +14,9 @@
 CROSS_CORR = 0.5
 NUGGET = 0.1
 BLOCK = 32
+GROUP = 4
+LANES = 128
+TINY = 1e-30
 
 
 def swapped(array):
@@ -22,31 +25,48 @@
 
 def eliminate(steps, gram_ref, upper_ref, inverse_ref, work_ref):
     count, rows, width = gram_ref.shape
-    lanes = lax.broadcasted_iota(jnp.int32, (1, width), 1)
+    lanes = lax.broadcasted_iota(jnp.int32, (1, 1, width), 2)
     work_ref[...] = gram_ref[:, :steps, :]
     if steps < rows:
         upper_ref[:, steps:, :] = jnp.zeros((count, rows - steps, width), jnp.float32)
         inverse_ref[:, steps:, :] = jnp.zeros((count, rows - steps, width), jnp.float32)
 
     for start in range(0, steps, BLOCK):
-
-        def step(k, carry, start=start):
-            here = lanes == k
-            for b in range(count):
-                row = work_ref[b, pl.ds(k, 1), :]
-                below = work_ref[b, start:, :]
-                pivot = jnp.sum(jnp.where(here, row, 0.0), axis=1, keepdims=True)
-                column = jnp.sum(jnp.where(here, below, 0.0), axis=1, keepdims=True)
+        tile = start // LANES * LANES
+
+        def step(turn, carry, start=start, tile=tile):
+            first = start + turn * GROUP
+            here = [lanes == first + i for i in range(GROUP)]
+            spot = [mark[:, :, tile : tile + LANES] for mark in here]
+            below = work_ref[:, start:, :]
+            rows = [work_ref[:, pl.ds(first + i, 1), :] for i in range(GROUP)]
+
+            def pick(values, i):
+                values = values[:, :, tile : tile + LANES]
+                return jnp.sum(jnp.where(spot[i], values, 0.0), axis=2, keepdims=True)
+
+            columns = [pick(below, i) for i in range(GROUP)]
+            corner = [[pick(rows[i], j) if j >= i else None for j in range(GROUP)] for i in range(GROUP)]
+            for i in range(GROUP):
+                pivot, row = corner[i][i], rows[i]
                 root = lax.rsqrt(pivot)
                 root = root * (1.5 - 0.5 * pivot * root * root)
-                upper_ref[b, pl.ds(k, 1), :] = jnp.where(lanes >= k, row, 0.0) * root
-                one = jnp.where(here, 1.0, 0.0)
-                inverse_ref[b, pl.ds(k, 1), :] = jnp.where(lanes < k, row, one) * root
-                scaled = column * (root * root)
-                work_ref[b, start:, :] = jnp.where(here, -scaled, below - scaled * row)
+                recip = root * root
+                upper_ref[:, pl.ds(first + i, 1), :] = jnp.where(lanes >= first + i, row, 0.0) * root
+                one = jnp.where(here[i], 1.0, 0.0)
+                inverse_ref[:, pl.ds(first + i, 1), :] = jnp.where(lanes < first + i, row, one) * root
+                scaled = columns[i] * recip
+                below = jnp.where(here[i], -scaled, below - scaled * row)
+                for j in range(i + 1, GROUP):
+                    ratio = corner[i][j] * recip
+                    rows[j] = jnp.where(here[i], -ratio, rows[j] - ratio * row)
+                    columns[j] = columns[j] - scaled * corner[i][j]
+                    for m in range(j, GROUP):
+                        corner[j][m] = corner[j][m] - ratio * corner[i][m]
+            work_ref[:, start:, :] = below
             return carry
 
-        lax.fori_loop(start, start + BLOCK, step, 0)
+        lax.fori_loop(0, BLOCK // GROUP, step, 0)
 
 
 def factor(gram, steps):
@@ -80,7 +100,8 @@
     far = far_ref[0]
     across = near[:, 0:1] - far[0:1, :]
     upward = near[:, 1:2] - far[1:2, :]
-    scaled = RANGE_SCALE * jnp.sqrt(across * across + upward * upward)
+    square = across * across + upward * upward
+    scaled = RANGE_SCALE * square * lax.rsqrt(jnp.maximum(square, TINY))
     decays = jnp.exp(-scaled)
     one = SIGMA_ONE * SIGMA_ONE * decays
     middle = (CROSS_CORR * SIGMA_ONE * SIGMA_TWO) * (1.0 + scaled) * decays
@@ -176,6 +197,12 @@
     bases = jnp.einsum(
         "lvnk,ljk->lvnj", local, every, precision=HIGHEST, preferred_element_type=jnp.float32
     )
+
+    leaf_share = rank_width // gens
+    leaf_pack = blocks.reshape(owned, gens, leaf_share, rank_width).transpose(1, 0, 2, 3)
+    leaf_pack = lax.all_to_all(leaf_pack, "gen", split_axis=0, concat_axis=0, tiled=True)
+    leaf_out = leaf_pack.reshape(gens, sides, each, leaf_share, rank_width)
+    leaf_out = leaf_out.transpose(1, 0, 2, 3, 4).reshape(leaf_count, leaf_share, rank_width)
 
     given = jnp.concatenate([factors, blocks, inverse], 2)
     far = swapped(side(given, 1 - parity))
@@ -208,33 +235,26 @@
     mixed = jnp.einsum("lab,lbj->laj", parent_matrix, parent_bases, precision=HIGHEST)
     parent_blocks = jnp.einsum("lak,laj->lkj", parent_bases, mixed, precision=HIGHEST)
 
-    leaf_share = rank_width // gens
     basis_share = 2 * rank_width // gens
     parent_share = parent_width // gens
-    lanes = 128
-    tiles = parent_width // lanes
+    tiles = parent_width // LANES
 
     def packed(values, share):
-        values = values.reshape(each, gens, share, tiles, lanes)
-        return values.transpose(1, 0, 3, 2, 4).reshape(gens, each * tiles * share, lanes)
+        values = values.reshape(each, gens, share, tiles, LANES)
+        return values.transpose(1, 0, 3, 2, 4).reshape(gens, each * tiles * share, LANES)
 
     def unpacked(values, share):
-        values = values.reshape(gens * each, tiles, share, lanes)
+        values = values.reshape(gens * each, tiles, share, LANES)
         if sides == 1:
             values = lax.dynamic_slice_in_dim(values, parity * half, half, 0)
         return values.transpose(0, 2, 1, 3).reshape(half, share, parent_width)
 
-    leaf_pack = blocks.reshape(owned, gens, leaf_share, rank_width).transpose(1, 0, 2, 3)
-    leaf_pack = leaf_pack.reshape(gens, owned * leaf_share, rank_width)
     pack = jnp.concatenate(
-        [leaf_pack, packed(parent_bases, basis_share), packed(parent_blocks, parent_share)], 1
+        [packed(parent_bases, basis_share), packed(parent_blocks, parent_share)], 1
     )
     pack = lax.all_to_all(pack, "gen", split_axis=0, concat_axis=0, tiled=True)
-    first = owned * leaf_share
-    second = first + each * tiles * basis_share
-    leaf_out = pack[:, :first].reshape(gens, sides, each, leaf_share, rank_width)
-    leaf_out = leaf_out.transpose(1, 0, 2, 3, 4).reshape(leaf_count, leaf_share, rank_width)
-    basis_out = unpacked(pack[:, first:second], basis_share)
+    second = each * tiles * basis_share
+    basis_out = unpacked(pack[:, :second], basis_share)
     block_out = unpacked(pack[:, second:], parent_share)
     return (bases[:, None], leaf_out[:, None], basis_out[:, None], block_out[:, None])
 

time: 201 us -> 140 us (0.70)
  Pallas kernels: 112 us -> 53 us
  waiting for transfers between devices: 21.9 us -> 15.7 us
  starting transfers between devices: 10.3 us -> 13.6 us
    pallas_call x2, Pallas kernels: 89.5 us -> 30.9 us  [factor(): pl.pallas_call(functools.partial(eliminate, steps), out_shape=(shape, sha...]
    all_to_all x1, waiting for transfers between devices: 12.7 us -> 8.02 us  [per_device(): pack = lax.all_to_all(pack, 'gen', split_axis=0, concat_axis=0, tiled=True)]
    all_to_all x0 -> x1, starting transfers between devices: none -> 3.41 us  [per_device(): lax.all_to_all(leaf_pack, 'gen', split_axis=0, concat_axis=0, tiled=True)]
  transfers between devices with their start and end apart: 6 -> 7, of which waited for: 3 -> 2; matrix products, arithmetic and copies ran while one was open for 13% -> 20% of each run, Pallas kernels for 45% -> 22%
where the time goes in v2:
time: 140 us; the launch traced here: 139 us
  Pallas kernels  53 us (38%)
  local copies, waits for them, and re-layouts  17.8 us (13%)
  waiting for transfers between devices  15.7 us (11%)
  between operations  14.3 us (10%)
  matrix products  13.9 us (10%)
  starting transfers between devices  13.6 us (10%)
  other arithmetic  10.2 us (7%)
    pallas_call x2, Pallas kernels, factor(): pl.pallas_call(functools.partial(eliminate, steps), out_shape=(shape, sha...  30.9 us
    pallas_call x1, Pallas kernels, covariance(): pl.pallas_call(gather_covariance, grid=(count, points // tile), in_specs=...  22.1 us
    all_to_all x1, waiting for transfers between devices, per_device(): pack = lax.all_to_all(pack, 'gen', split_axis=0, concat_axis=0, tiled=True)  8.02 us
    all_to_all x1, waiting for transfers between devices, per_device(): lax.all_to_all(spread, 'gen', split_axis=1, concat_axis=4, tiled=True)  7.63 us
    all_to_all x1, starting transfers between devices, per_device(): lax.all_to_all(spread, 'gen', split_axis=1, concat_axis=4, tiled=True)  5.29 us
    all_to_all x1, starting transfers between devices, per_device(): pack = lax.all_to_all(pack, 'gen', split_axis=0, concat_axis=0, tiled=True)  4.43 us
    all_to_all x1, starting transfers between devices, per_device(): lax.all_to_all(leaf_pack, 'gen', split_axis=0, concat_axis=0, tiled=True)  3.41 us
    dot_general x2, matrix products, sandwich(): mixed = jnp.einsum('lab,lcb->lac', inner, right, precision=HIGHEST)  2.95 us
  transfers between devices with their start and end apart: 7, of which 2 were waited for; matrix products, arithmetic and copies ran while one was open for 20% of the time, Pallas kernels for 22%

profile of v2, /device:TPU:0, one launch (start us, length us, event | category | flops | bytes accessed | tf_op | source)
XLA Modules:
  0.0 138.6 jit_solution(9766625608092176652)
XLA Ops:
  7.2 2.4 %copy.66 = bf16[2,4,2,2,128,128]{5,4,3,2,0,1:T(8,128)(2,1)} copy(bf16[2,4,2,2,128,128]{5,4,3,2,1,0:T(8,128)(2,1)} %bitcast.78) | data formatting | bytes 2097152 | tf_op jit(solution)/shard_map/reshape;squeeze | solution.py:169
  9.6 5.3 %all-to-all-start = ((bf16[2,4,2,2,128,128]{5,4,3,2,0,1:T(8,128)(2,1)}), bf16[2,4,2,2,128,128]{5,4,3,2,0,1:T(8,128)(2,1)S(1)}, u32[]{:S(2)}, u32[]{:S(2)}) async-start(bf16[2,4,2,2,128,128]{5,4,3,2,0,1:T(8,128)(2,1)} %copy.66), calls=%async_computation | async-start | bytes 2097152 | tf_op jit(solution)/shard_map/all_to_all | solution.py:170
  19.2 1.7 %copy.71.near_ref = f32[6,512,2]{2,1,0:T(8,128)} copy(f32[6,512,2]{1,2,0:T(2,128)S(1)} %get-tuple-element.43) | data formatting | bytes 49152 | tf_op jit(solution)/shard_map/transpose | solution.py:136
  20.9 7.6 %all-to-all-done = bf16[2,4,2,2,128,128]{5,4,3,2,0,1:T(8,128)(2,1)S(1)} async-done(((bf16[2,4,2,2,128,128]{5,4,3,2,0,1:T(8,128)(2,1)}), bf16[2,4,2,2,128,128]{5,4,3,2,0,1:T(8,128)(2,1)S(1)}, u32[]{:S(2)}, u32[]{:S(2)}) %all-to-all-start) | async-done | bytes 1048608 | tf_op jit(solution)/shard_map/all_to_all | solution.py:170
  29.5 1.3 multiply_add_fusion
  30.8 15.9 %shard_map.84 = (f32[4,128,128]{2,1,0:T(8,128)}, f32[4,128,128]{2,1,0:T(8,128)}) custom-call(f32[4,128,128]{2,1,0:T(8,128)} %get-tuple-element.46.gram_ref), custom_call_target="tpu_custom_call" | custom-call | tf_op jit(solution)/shard_map/pallas_call | solution.py:75
  46.7 1.1 broadcast_multiply_fusion
  47.8 1.5 %fusion.15 = f32[4,128,256]{2,1,0:T(8,128)S(1)} fusion(bf16[4,128,256]{2,1,0:T(8,128)(2,1)} %bitcast.86, f32[4,128,128]{2,1,0:T(8,128)} %get-tuple-element.8, f32[4,128]{1,0:T(4,128)S(1)} %fusion.27), kind=kOutput, calls=%fused_computation.28 | convolution fusion | flops 201392128 | bytes 1050624 | tf_op jit(solution)/shard_map/lkj,ljp->lkp/dot_general | solution.py:187
  49.3 2.9 %pad_maximum_fusion = (bf16[6,2,512,128]{3,2,1,0:T(8,128)(2,1)}, bf16[6,2,512,128]{3,2,1,0:T(8,128)(2,1)}) fusion(bf16[4,2,512,128]{3,2,1,0:T(8,128)(2,1)S(1)} %bitcast.75, bf16[2,2,512,128]{3,2,1,0:T(8,128)(2,1)} %collective-permute-done.1, bf16[2,2,512,128]{3,2,1,0:T(8,128)(2,1)S(1)} %get-tuple-element.37), kind=kLoop, calls=%fused_computation | loop fusion | flops 1572864 | bytes 5242880 | tf_op jit(solution)/shard_map/concatenate | solution.py:194
  52.3 22.1 %shard_map.85 = f32[6,128,128]{2,1,0:T(8,128)} custom-call(f32[6,512,2]{2,1,0:T(8,128)} %copy.71.near_ref, f32[6,2,512]{2,1,0:T(2,128)} %get-tuple-element.42.far_ref, bf16[6,2,512,128]{3,2,1,0:T(8,128)(2,1)} %get-tuple-element.35.near_rows_ref, bf16[6,2,512,128]{3,2,1,0:T(8,128)(2,1)} %get-tuple-element.34.far_rows_ref), custom_call_target="tpu_custom_call" | custom-call | tf_op jit(solution)/shard_map/pallas_call | solution.py:125
  74.4 1.6 %fusion.12 = f32[4,128,128]{2,1,0:T(8,128)S(1)} fusion(f32[4,128,128]{2,1,0:T(8,128)S(1)} %broadcast_multiply_fusion, f32[6,128,128]{2,1,0:T(8,128)} %shard_map.85, f32[4,128,128]{2,1,0:T(8,128)S(1)} %copy-done.5), kind=kOutput, calls=%fused_computation.23 | convolution fusion | flops 100794368 | bytes 1048576 | tf_op jit(solution)/shard_map/lab,lcb->lac/dot_general | solution.py:140
  78.8 3.4 %all-to-all-start.1 = ((f32[4,4,32,128]{3,2,1,0:T(8,128)}), f32[4,4,32,128]{3,2,1,0:T(8,128)S(1)}, u32[]{:S(2)}, u32[]{:S(2)}) async-start(f32[4,4,32,128]{3,2,1,0:T(8,128)} %bitcast.71), calls=%async_computation.1 | async-start | bytes 524288 | tf_op jit(solution)/shard_map/all_to_all | solution.py:203
  82.2 1.3 fusion.19
  86.6 1.9 %convolution_add_fusion.gram_ref = f32[2,256,256]{2,1,0:T(8,128)} fusion(f32[2,128,256]{2,1,0:T(8,128)S(1)} %get-tuple-element.33, f32[2,128,256]{2,1,0:T(8,128)S(1)} %get-tuple-element.32, f32[2,256]{1,0:T(2,128)S(1)} %broadcast_subtract_fusion, f32[256,256]{1,0:T(8,128)S(1)} %copy-done.4, f32[2,256]{1,0:T(2,128)S(1)} %compare_convert_fusion), kind=kOutput, calls=%fused_computation.3 | convolution fusion | flops 403177472 | bytes 1314816 | tf_op jit(solution)/shard_map/lak,laj->lkj/dot_general | solution.py:228
  88.5 15.0 %shard_map.86 = (f32[2,256,256]{2,1,0:T(8,128)}, f32[2,256,256]{2,1,0:T(8,128)}) custom-call(f32[2,256,256]{2,1,0:T(8,128)} %convolution_add_fusion.gram_ref), custom_call_target="tpu_custom_call" | custom-call | tf_op jit(solution)/shard_map/pallas_call | solution.py:75
  103.5 1.7 %fusion.11 = f32[2,256,256]{2,1,0:T(8,128)S(1)} fusion(f32[2,256,256]{2,1,0:T(8,128)} %get-tuple-element.9, f32[2,128,256]{2,1,0:T(8,128)S(1)} %get-tuple-element.33, f32[2,128,256]{2,1,0:T(8,128)S(1)} %get-tuple-element.32, f32[2,256]{1,0:T(2,128)S(1)} %compare_convert_fusion), kind=kOutput, calls=%fused_computation.21 | convolution fusion | flops 402915328 | bytes 1574912 | tf_op jit(solution)/shard_map/lak,ljk->laj/dot_general | solution.py:231
  108.7 4.4 %all-to-all-start.2 = ((f32[4,512,128]{2,1,0:T(8,128)}), f32[4,512,128]{2,1,0:T(8,128)}, u32[]{:S(2)}, u32[]{:S(2)}) async-start(f32[4,512,128]{2,1,0:T(8,128)} %pad_maximum_fusion.2), calls=%async_computation.2 | async-start | bytes 2097152 | tf_op jit(solution)/shard_map/all_to_all | solution.py:255
  113.9 1.3 copy.69
  115.2 2.2 %convolution_bitcast_fusion = f32[16,1,2,128,128]{3,4,2,0,1:T(8,128)S(1)} fusion(f32[16,128,128,1]{2,1,3,0:T(8,128)S(1)} %bitcast.79, bf16[16,1,2,128,128]{4,3,2,1,0:T(8,128)(2,1)} %param.6), kind=kOutput, calls=%fused_computation.2 | convolution fusion | flops 805306368 | bytes 4194304 | tf_op jit(solution)/shard_map/lvnk,ljk->lvnj/dot_general | solution.py:197
  117.4 1.8 %copy.82 = f32[16,1,2,128,128]{4,3,2,1,0:T(8,128)} copy(f32[16,1,2,128,128]{3,4,2,0,1:T(8,128)S(1)} %convolution_bitcast_fusion) | data formatting | bytes 4194304
  119.2 8.0 %all-to-all-done.2 = f32[4,512,128]{2,1,0:T(8,128)} async-done(((f32[4,512,128]{2,1,0:T(8,128)}), f32[4,512,128]{2,1,0:T(8,128)}, u32[]{:S(2)}, u32[]{:S(2)}) %all-to-all-start.2) | async-done | bytes 1048608 | tf_op jit(solution)/shard_map/all_to_all | solution.py:255
  127.2 1.3 fusion.34
  128.9 1.2 broadcast_in_dim_reshape.11
  130.5 1.2 broadcast_in_dim_reshape.12
  (61 shorter events, 16.0 us)
Async XLA Ops:
  7.2 10.5 %copy-start = (bf16[16,1,128,256]{3,2,1,0:T(8,128)(2,1)S(1)}, bf16[16,1,128,256]{3,2,1,0:T(8,128)(2,1)}, u32[]{:S(2)}) copy-start(bf16[16,1,128,256]{3,2,1,0:T(8,128)(2,1)} %param.8) | copy-start | bytes 3145732
  9.6 7.3 %copy-start.6 = (s32[16,1]{0,1:T(1,128)S(1)}, s32[16,1]{0,1:T(1,128)}, u32[]{:S(2)}) copy-start(s32[16,1]{0,1:T(1,128)} %param.7) | copy-start | bytes 196
  9.6 18.9 %all-to-all-start = ((bf16[2,4,2,2,128,128]{5,4,3,2,0,1:T(8,128)(2,1)}), bf16[2,4,2,2,128,128]{5,4,3,2,0,1:T(8,128)(2,1)S(1)}, u32[]{:S(2)}, u32[]{:S(2)}) async-start(bf16[2,4,2,2,128,128]{5,4,3,2,0,1:T(8,128)(2,1)} %copy.66), calls=%async_computation | async-start | bytes 2097152 | tf_op jit(solution)/shard_map/all_to_all | solution.py:170
  14.9 99.0 %all-gather.2.cloned.1.call-start = ((), (), s32[]{:S(2)}) async-start(), calls=%async_computation.3 | async-start | bytes 1310720 | tf_op jit(solution)/shard_map/all_gather | solution.py:184
  15.6 3.0 %collective-permute-start = (f32[2,2,512]{2,1,0:T(2,128)S(1)}, f32[2,2,512]{2,1,0:T(2,128)S(1)}, u32[]{:S(2)}, u32[]{:S(2)}) collective-permute-start(f32[2,2,512]{2,1,0:T(2,128)S(1)} %get-tuple-element.44), channel_id=1, source_target_pairs={{0,4},{4,0},{8,12},{12,8},{16,20},{20,16},{24,28},{28,24},{1,5},{5... | collective-permute-start | bytes 24584 | tf_op jit(solution)/shard_map/ppermute | solution.py:23
  29.5 19.8 %collective-permute-start.1 = (bf16[2,2,512,128]{3,2,1,0:T(8,128)(2,1)}, bf16[2,2,512,128]{3,2,1,0:T(8,128)(2,1)}, u32[]{:S(2)}, u32[]{:S(2)}) collective-permute-start(bf16[2,2,512,128]{3,2,1,0:T(8,128)(2,1)} %get-tuple-element.36), channel_id=1, source_target_pairs={{0,4},{4,0},{8,12},{12,8},{16,20},{20,16},{24,28},{28,24},{1,5},{5... | collective-permute-start | bytes 1572872 | tf_op jit(solution)/shard_map/ppermute | solution.py:23
  47.8 28.6 %copy-start.1 = (f32[4,128,128]{2,1,0:T(8,128)}, f32[4,128,128]{2,1,0:T(8,128)S(1)}, u32[]{:S(2)}) copy-start(f32[4,128,128]{2,1,0:T(8,128)S(1)} %broadcast_multiply_fusion) | copy-start | bytes 786436
  52.3 22.1 %copy-start.5 = (f32[4,128,128]{2,1,0:T(8,128)S(1)}, f32[4,128,128]{2,1,0:T(8,128)}, u32[]{:S(2)}) copy-start(f32[4,128,128]{2,1,0:T(8,128)} %get-tuple-element.47) | copy-start | bytes 786436
  74.4 3.4 %copy-start.7 = (s32[8,1]{0,1:T(1,128)S(1)}, s32[8,1]{0,1:T(1,128)}, u32[]{:S(2)}) copy-start(s32[8,1]{0,1:T(1,128)} %param.9) | copy-start | bytes 100
  76.4 5.8 %copy-start.3 = (f32[6,128,128]{2,1,0:T(8,128)S(1)}, f32[6,128,128]{2,1,0:T(8,128)}, u32[]{:S(2)}) copy-start(f32[6,128,128]{2,1,0:T(8,128)} %shard_map.85) | copy-start | bytes 1179652
  77.3 6.3 %copy-start.2 = (f32[4,128,128]{2,1,0:T(8,128)S(1)}, f32[4,128,128]{2,1,0:T(8,128)}, u32[]{:S(2)}) copy-start(f32[4,128,128]{2,1,0:T(8,128)} %copy-done.1) | copy-start | bytes 786436
  77.3 4.9 %collective-permute-start.2 = (f32[2,128,512]{2,1,0:T(8,128)}, f32[2,128,512]{2,1,0:T(8,128)}, u32[]{:S(2)}, u32[]{:S(2)}) collective-permute-start(f32[2,128,512]{2,1,0:T(8,128)} %fusion.2), channel_id=1, source_target_pairs={{0,4},{4,0},{8,12},{12,8},{16,20},{20,16},{24,28},{28,24},{1,5},{5... | collective-permute-start | bytes 1572872 | tf_op jit(solution)/shard_map/ppermute | solution.py:23
  78.8 29.9 %all-to-all-start.1 = ((f32[4,4,32,128]{3,2,1,0:T(8,128)}), f32[4,4,32,128]{3,2,1,0:T(8,128)S(1)}, u32[]{:S(2)}, u32[]{:S(2)}) async-start(f32[4,4,32,128]{3,2,1,0:T(8,128)} %bitcast.71), calls=%async_computation.1 | async-start | bytes 524288 | tf_op jit(solution)/shard_map/all_to_all | solution.py:203
  82.2 4.4 %copy-start.4 = (f32[256,256]{1,0:T(8,128)S(1)}, f32[256,256]{1,0:T(8,128)}, u32[]{:S(2)}) copy-start(f32[256,256]{1,0:T(8,128)} %fusion.18) | copy-start | bytes 786436
  108.7 18.5 %all-to-all-start.2 = ((f32[4,512,128]{2,1,0:T(8,128)}), f32[4,512,128]{2,1,0:T(8,128)}, u32[]{:S(2)}, u32[]{:S(2)}) async-start(f32[4,512,128]{2,1,0:T(8,128)} %pad_maximum_fusion.2), calls=%async_computation.2 | async-start | bytes 2097152 | tf_op jit(solution)/shard_map/all_to_all | solution.py:255
Sparse Core Ops, SparseCore 0:
  78.2 26.9 all-gather.1

commit v3 on v2

--- a/solution.py
+++ b/solution.py
@@ -16,6 +16,7 @@
 BLOCK = 32
 GROUP = 4
 LANES = 128
+TILE = 512
 TINY = 1e-30
 
 
@@ -121,7 +122,7 @@
 
 def covariance(near_coords, far_coords, near_rows, far_rows):
     count, _, points, width = near_rows.shape
-    tile = 128
+    tile = min(TILE, points)
     return pl.pallas_call(
         gather_covariance,
         grid=(count, points // tile),
@@ -187,13 +188,9 @@
     factors = jnp.einsum(
         "lkj,ljp->lkp", upper, mine(translations[:, 0]).astype(jnp.float32), precision=HIGHEST
     )
-    sums = covariance(
-        jnp.concatenate([coords, side(coords, parity)], 0),
-        jnp.concatenate([coords, far_coords], 0),
-        jnp.concatenate([rows, side(rows, parity)], 0),
-        jnp.concatenate([rows, far_rows], 0),
-    )
-    blocks = sandwich(inverse, sums[:owned] + NUGGET * full, inverse)
+    sums = covariance(coords, coords, rows, rows)
+    crossed = covariance(side(coords, parity), far_coords, side(rows, parity), far_rows)
+    blocks = sandwich(inverse, sums + NUGGET * full, inverse)
     bases = jnp.einsum(
         "lvnk,ljk->lvnj", local, every, precision=HIGHEST, preferred_element_type=jnp.float32
     )
@@ -210,7 +207,7 @@
     far_factor = far[:, :, :parent_width]
     far_block = far[:, :, parent_width : parent_width + rank_width]
     far_inverse = far[:, :, parent_width + rank_width :]
-    coupled = sandwich(side(inverse, parity), sums[owned:], far_inverse)
+    coupled = sandwich(side(inverse, parity), crossed, far_inverse)
     coupled = jnp.where(is_even, coupled, jnp.swapaxes(coupled, 1, 2))
     even_block = jnp.where(is_even, own_block, far_block)
     odd_block = jnp.where(is_even, far_block, own_block)
@@ -237,23 +234,22 @@
 
     basis_share = 2 * rank_width // gens
     parent_share = parent_width // gens
-    tiles = parent_width // LANES
 
     def packed(values, share):
-        values = values.reshape(each, gens, share, tiles, LANES)
-        return values.transpose(1, 0, 3, 2, 4).reshape(gens, each * tiles * share, LANES)
+        values = values.reshape(each, gens, share, parent_width)
+        return values.transpose(1, 0, 2, 3).reshape(gens, each * share, parent_width)
 
     def unpacked(values, share):
-        values = values.reshape(gens * each, tiles, share, LANES)
+        values = values.reshape(gens * each, share, parent_width)
         if sides == 1:
             values = lax.dynamic_slice_in_dim(values, parity * half, half, 0)
-        return values.transpose(0, 2, 1, 3).reshape(half, share, parent_width)
+        return values
 
     pack = jnp.concatenate(
         [packed(parent_bases, basis_share), packed(parent_blocks, parent_share)], 1
     )
     pack = lax.all_to_all(pack, "gen", split_axis=0, concat_axis=0, tiled=True)
-    second = each * tiles * basis_share
+    second = each * basis_share
     basis_out = unpacked(pack[:, :second], basis_share)
     block_out = unpacked(pack[:, second:], parent_share)
     return (bases[:, None], leaf_out[:, None], basis_out[:, None], block_out[:, None])

time: 140 us -> 132 us (0.943)
  waiting for transfers between devices: 15.7 us -> 23.2 us
  Pallas kernels: 53 us -> 46.6 us
  other arithmetic: 10.2 us -> 5.89 us
  local copies, waits for them, and re-layouts: 17.8 us -> 14.8 us
    pallas_call x1 -> x2, Pallas kernels: 22.1 us -> 15.7 us  [covariance(): pl.pallas_call(gather_covariance, grid=(count, points // tile), in_specs=...]
    all_to_all x1, waiting for transfers between devices: 8.02 us -> 12.8 us  [per_device(): pack = lax.all_to_all(pack, 'gen', split_axis=0, concat_axis=0, tiled=True)]
    concatenate x2 -> x0, other arithmetic: 3.53 us -> none  [the longest x1 2.91 us: per_device(): jnp.concatenate([rows, far_rows], 0)]
    another operation x2 -> x0, local copies, waits for them, and re-layouts: 2.43 us -> none  [the longest x1 1.21 us: per_device(): basis_out[:, None]]
    all_to_all x1, waiting for transfers between devices: 7.63 us -> 9.87 us  [per_device(): lax.all_to_all(spread, 'gen', split_axis=1, concat_axis=4, tiled=True)]
    unnamed x18 -> x22, local copies, waits for them, and re-layouts: 2.36 us -> 3.74 us
  transfers between devices with their start and end apart: 7 -> 7, of which waited for: 2 -> 2; matrix products, arithmetic and copies ran while one was open for 20% -> 18% of each run, Pallas kernels for 22% -> 36%
where the time goes in v3:
time: 132 us; the launch traced here: 131 us
  Pallas kernels  46.6 us (35%)
  waiting for transfers between devices  23.2 us (18%)
  local copies, waits for them, and re-layouts  14.8 us (11%)
  between operations  14.3 us (11%)
  starting transfers between devices  13.6 us (10%)
  matrix products  12.7 us (10%)
  other arithmetic  5.89 us (4%)
    pallas_call x2, Pallas kernels, factor(): pl.pallas_call(functools.partial(eliminate, steps), out_shape=(shape, sha...  30.9 us
    pallas_call x2, Pallas kernels, covariance(): pl.pallas_call(gather_covariance, grid=(count, points // tile), in_specs=...  15.7 us
    all_to_all x1, waiting for transfers between devices, per_device(): pack = lax.all_to_all(pack, 'gen', split_axis=0, concat_axis=0, tiled=True)  12.8 us
    all_to_all x1, waiting for transfers between devices, per_device(): lax.all_to_all(spread, 'gen', split_axis=1, concat_axis=4, tiled=True)  9.87 us
    all_to_all x1, starting transfers between devices, per_device(): lax.all_to_all(spread, 'gen', split_axis=1, concat_axis=4, tiled=True)  5.29 us
    all_to_all x1, starting transfers between devices, per_device(): pack = lax.all_to_all(pack, 'gen', split_axis=0, concat_axis=0, tiled=True)  4.14 us
    unnamed x22, local copies, waits for them, and re-layouts  3.74 us
    all_to_all x1, starting transfers between devices, per_device(): lax.all_to_all(leaf_pack, 'gen', split_axis=0, concat_axis=0, tiled=True)  3.41 us
  transfers between devices with their start and end apart: 7, of which 2 were waited for; matrix products, arithmetic and copies ran while one was open for 18% of the time, Pallas kernels for 36%

profile of v3, /device:TPU:0, one launch (start us, length us, event | category | flops | bytes accessed | tf_op | source)
XLA Modules:
  0.0 131.0 jit_solution(3846574835046272305)
XLA Ops:
  7.2 2.4 %copy.52 = bf16[2,4,2,2,128,128]{5,4,3,2,0,1:T(8,128)(2,1)} copy(bf16[2,4,2,2,128,128]{5,4,3,2,1,0:T(8,128)(2,1)} %bitcast.83) | data formatting | bytes 2097152 | tf_op jit(solution)/shard_map/reshape;squeeze | solution.py:170
  9.6 5.3 %all-to-all-start = ((bf16[2,4,2,2,128,128]{5,4,3,2,0,1:T(8,128)(2,1)}), bf16[2,4,2,2,128,128]{5,4,3,2,0,1:T(8,128)(2,1)S(1)}, u32[]{:S(2)}, u32[]{:S(2)}) async-start(bf16[2,4,2,2,128,128]{5,4,3,2,0,1:T(8,128)(2,1)} %copy.52), calls=%async_computation | async-start | bytes 2097152 | tf_op jit(solution)/shard_map/all_to_all | solution.py:171
  17.0 1.4 %copy.57.near_ref = f32[4,512,2]{2,1,0:T(8,128)} copy(f32[4,512,2]{1,2,0:T(2,128)S(1)} %bitcast.94) | data formatting | bytes 32768 | tf_op jit(solution)/shard_map/transpose | solution.py:137
  18.7 9.9 %all-to-all-done = bf16[2,4,2,2,128,128]{5,4,3,2,0,1:T(8,128)(2,1)S(1)} async-done(((bf16[2,4,2,2,128,128]{5,4,3,2,0,1:T(8,128)(2,1)}), bf16[2,4,2,2,128,128]{5,4,3,2,0,1:T(8,128)(2,1)S(1)}, u32[]{:S(2)}, u32[]{:S(2)}) %all-to-all-start) | async-done | bytes 1048608 | tf_op jit(solution)/shard_map/all_to_all | solution.py:171
  28.6 1.1 constant_dynamic-slice_fusion
  29.8 1.2 multiply_add_fusion
  31.0 15.9 %shard_map.84 = (f32[4,128,128]{2,1,0:T(8,128)}, f32[4,128,128]{2,1,0:T(8,128)}) custom-call(f32[4,128,128]{2,1,0:T(8,128)} %get-tuple-element.38.gram_ref), custom_call_target="tpu_custom_call" | custom-call | tf_op jit(solution)/shard_map/pallas_call | solution.py:76
  46.9 1.1 broadcast_multiply_fusion
  48.0 9.9 %shard_map.85 = f32[4,128,128]{2,1,0:T(8,128)} custom-call(f32[4,512,2]{2,1,0:T(8,128)} %copy.57.near_ref, f32[4,2,512]{2,1,0:T(2,128)} %bitcast.95, bf16[4,2,512,128]{3,2,1,0:T(8,128)(2,1)} %bitcast.78, bf16[4,2,512,128]{3,2,1,0:T(8,128)(2,1)} %bitcast.79), custom_call_target="tpu_custom_call" | custom-call | tf_op jit(solution)/shard_map/pallas_call | solution.py:126
  57.9 1.6 %fusion.16 = f32[4,128,128]{2,1,0:T(8,128)S(1)} fusion(f32[4,128,128]{2,1,0:T(8,128)S(1)} %broadcast_multiply_fusion, f32[4,128,128]{2,1,0:T(8,128)} %shard_map.85, f32[4,128,128]{2,1,0:T(8,128)S(1)} %get-tuple-element.39), kind=kOutput, calls=%fused_computation.26 | convolution fusion | flops 100794368 | bytes 1048576 | tf_op jit(solution)/shard_map/lab,lcb->lac/dot_general | solution.py:141
  63.6 3.4 %all-to-all-start.1 = ((f32[4,4,32,128]{3,2,1,0:T(8,128)}), f32[4,4,32,128]{3,2,1,0:T(8,128)S(1)}, u32[]{:S(2)}, u32[]{:S(2)}) async-start(f32[4,4,32,128]{3,2,1,0:T(8,128)} %bitcast.74), calls=%async_computation.1 | async-start | bytes 524288 | tf_op jit(solution)/shard_map/all_to_all | solution.py:200
  68.4 5.8 %shard_map.87 = f32[2,128,128]{2,1,0:T(8,128)} custom-call(f32[2,512,2]{2,1,0:T(8,128)} %copy.63.near_ref, f32[2,2,512]{2,1,0:T(2,128)} %copy-done.7, bf16[2,2,512,128]{3,2,1,0:T(8,128)(2,1)} %get-tuple-element.29.near_rows_ref, bf16[2,2,512,128]{3,2,1,0:T(8,128)(2,1)} %collective-permute-done.2.far_rows_ref), custom_call_target="tpu_custom_call" | custom-call | tf_op jit(solution)/shard_map/pallas_call | solution.py:126
  75.0 1.3 fusion.20
  77.7 1.9 %convolution_add_fusion.gram_ref = f32[2,256,256]{2,1,0:T(8,128)} fusion(f32[2,128,256]{2,1,0:T(8,128)S(1)} %get-tuple-element.31, f32[2,128,256]{2,1,0:T(8,128)S(1)} %get-tuple-element.30, f32[2,256]{1,0:T(2,128)S(1)} %broadcast_subtract_fusion, f32[256,256]{1,0:T(8,128)S(1)} %fusion.19, f32[2,256]{1,0:T(2,128)S(1)} %compare_convert_fusion), kind=kOutput, calls=%fused_computation.1 | convolution fusion | flops 403177472 | bytes 1314816 | tf_op jit(solution)/shard_map/lak,laj->lkj/dot_general | solution.py:225
  79.5 15.0 %shard_map.86 = (f32[2,256,256]{2,1,0:T(8,128)}, f32[2,256,256]{2,1,0:T(8,128)}) custom-call(f32[2,256,256]{2,1,0:T(8,128)} %convolution_add_fusion.gram_ref), custom_call_target="tpu_custom_call" | custom-call | tf_op jit(solution)/shard_map/pallas_call | solution.py:76
  94.6 1.7 %fusion.11 = f32[2,256,256]{2,1,0:T(8,128)S(1)} fusion(f32[2,256,256]{2,1,0:T(8,128)} %get-tuple-element.9, f32[2,128,256]{2,1,0:T(8,128)S(1)} %get-tuple-element.31, f32[2,128,256]{2,1,0:T(8,128)S(1)} %get-tuple-element.30, f32[2,256]{1,0:T(2,128)S(1)} %compare_convert_fusion), kind=kOutput, calls=%fused_computation.19 | convolution fusion | flops 402915328 | bytes 1574912 | tf_op jit(solution)/shard_map/lak,ljk->laj/dot_general | solution.py:228
  97.9 1.0 fusion.37
  99.0 1.0 pad_maximum_fusion
  100.1 4.1 %all-to-all-start.2 = ((f32[4,256,256]{2,1,0:T(8,128)}), f32[4,256,256]{2,1,0:T(8,128)S(1)}, u32[]{:S(2)}, u32[]{:S(2)}) async-start(f32[4,256,256]{2,1,0:T(8,128)} %pad_maximum_fusion), calls=%async_computation.2 | async-start | bytes 2097152 | tf_op jit(solution)/shard_map/all_to_all | solution.py:251
  104.9 12.8 %all-to-all-done.2 = f32[4,256,256]{2,1,0:T(8,128)S(1)} async-done(((f32[4,256,256]{2,1,0:T(8,128)}), f32[4,256,256]{2,1,0:T(8,128)S(1)}, u32[]{:S(2)}, u32[]{:S(2)}) %all-to-all-start.2) | async-done | bytes 1048608 | tf_op jit(solution)/shard_map/all_to_all | solution.py:251
  117.8 1.1 fusion.35
  118.8 1.3 copy.55
  120.1 2.2 %convolution_bitcast_fusion = f32[16,1,2,128,128]{3,4,2,0,1:T(8,128)S(1)} fusion(f32[16,128,128,1]{2,1,3,0:T(8,128)S(1)} %bitcast.84, bf16[16,1,2,128,128]{4,3,2,1,0:T(8,128)(2,1)} %param.6), kind=kOutput, calls=%fused_computation | convolution fusion | flops 805306368 | bytes 4194304 | tf_op jit(solution)/shard_map/lvnk,ljk->lvnj/dot_general | solution.py:194
  122.4 1.8 %copy.67 = f32[16,1,2,128,128]{4,3,2,1,0:T(8,128)} copy(f32[16,1,2,128,128]{3,4,2,0,1:T(8,128)S(1)} %convolution_bitcast_fusion) | data formatting | bytes 4194304
  (60 shorter events, 12.4 us)
Async XLA Ops:
  7.2 11.3 %copy-start = (bf16[16,1,128,256]{3,2,1,0:T(8,128)(2,1)S(1)}, bf16[16,1,128,256]{3,2,1,0:T(8,128)(2,1)}, u32[]{:S(2)}) copy-start(bf16[16,1,128,256]{3,2,1,0:T(8,128)(2,1)} %param.8) | copy-start | bytes 3145732
  7.2 9.0 %copy-start.8 = (s32[16,1]{0,1:T(1,128)S(1)}, s32[16,1]{0,1:T(1,128)}, u32[]{:S(2)}) copy-start(s32[16,1]{0,1:T(1,128)} %param.7) | copy-start | bytes 196
  9.6 8.8 %copy-start.9 = (s32[8,1]{0,1:T(1,128)S(1)}, s32[8,1]{0,1:T(1,128)}, u32[]{:S(2)}) copy-start(s32[8,1]{0,1:T(1,128)} %param.9) | copy-start | bytes 100
  9.6 18.9 %all-to-all-start = ((bf16[2,4,2,2,128,128]{5,4,3,2,0,1:T(8,128)(2,1)}), bf16[2,4,2,2,128,128]{5,4,3,2,0,1:T(8,128)(2,1)S(1)}, u32[]{:S(2)}, u32[]{:S(2)}) async-start(bf16[2,4,2,2,128,128]{5,4,3,2,0,1:T(8,128)(2,1)} %copy.52), calls=%async_computation | async-start | bytes 2097152 | tf_op jit(solution)/shard_map/all_to_all | solution.py:171
  15.6 14.2 %copy-start.5 = (f32[2,1,2,2,512]{4,3,2,1,0:T(2,128)}, f32[2,1,2,2,512]{4,3,2,1,0:T(2,128)S(1)}, u32[]{:S(2)}) copy-start(f32[2,1,2,2,512]{4,3,2,1,0:T(2,128)S(1)} %constant_dynamic-slice_fusion.5) | copy-start | bytes 49156
  15.6 52.2 %collective-permute-start.1 = (f32[2,2,512]{2,1,0:T(2,128)S(1)}, f32[2,2,512]{2,1,0:T(2,128)S(1)}, u32[]{:S(2)}, u32[]{:S(2)}) collective-permute-start(f32[2,2,512]{2,1,0:T(2,128)S(1)} %get-tuple-element.36), channel_id=1, source_target_pairs={{0,4},{4,0},{8,12},{12,8},{16,20},{20,16},{24,28},{28,24},{1,5},{5... | collective-permute-start | bytes 24584 | tf_op jit(solution)/shard_map/ppermute | solution.py:24
  28.6 2.4 %copy-start.1 = (bf16[2,1,2,2,4,128,128]{6,5,4,3,2,0,1:T(8,128)(2,1)}, bf16[2,1,2,2,4,128,128]{6,5,4,3,2,0,1:T(8,128)(2,1)S(1)}, u32[]{:S(2)}) copy-start(bf16[2,1,2,2,4,128,128]{6,5,4,3,2,0,1:T(8,128)(2,1)S(1)} %copy.53) | copy-start | bytes 3145732
  48.0 12.4 %copy-start.2 = (f32[4,128,128]{2,1,0:T(8,128)}, f32[4,128,128]{2,1,0:T(8,128)S(1)}, u32[]{:S(2)}) copy-start(f32[4,128,128]{2,1,0:T(8,128)S(1)} %broadcast_multiply_fusion) | copy-start | bytes 786436
  48.0 12.0 %copy-start.6 = (f32[4,128,128]{2,1,0:T(8,128)S(1)}, f32[4,128,128]{2,1,0:T(8,128)}, u32[]{:S(2)}) copy-start(f32[4,128,128]{2,1,0:T(8,128)} %get-tuple-element.8) | copy-start | bytes 786436
  61.2 13.0 %collective-permute-start = (f32[2,128,512]{2,1,0:T(8,128)}, f32[2,128,512]{2,1,0:T(8,128)S(1)}, u32[]{:S(2)}, u32[]{:S(2)}) collective-permute-start(f32[2,128,512]{2,1,0:T(8,128)} %fusion.2), channel_id=1, source_target_pairs={{0,4},{4,0},{8,12},{12,8},{16,20},{20,16},{24,28},{28,24},{1,5},{5... | collective-permute-start | bytes 1572872 | tf_op jit(solution)/shard_map/ppermute | solution.py:24
  61.2 6.6 %collective-permute-start.2 = (bf16[2,2,512,128]{3,2,1,0:T(8,128)(2,1)}, bf16[2,2,512,128]{3,2,1,0:T(8,128)(2,1)}, u32[]{:S(2)}, u32[]{:S(2)}) collective-permute-start(bf16[2,2,512,128]{3,2,1,0:T(8,128)(2,1)} %get-tuple-element.28), channel_id=1, source_target_pairs={{0,4},{4,0},{8,12},{12,8},{16,20},{20,16},{24,28},{28,24},{1,5},{5... | collective-permute-start | bytes 1572872 | tf_op jit(solution)/shard_map/ppermute | solution.py:24
  61.9 14.4 %copy-start.3 = (f32[4,128,128]{2,1,0:T(8,128)S(1)}, f32[4,128,128]{2,1,0:T(8,128)}, u32[]{:S(2)}) copy-start(f32[4,128,128]{2,1,0:T(8,128)} %copy-done.2) | copy-start | bytes 786436
  63.6 36.4 %all-to-all-start.1 = ((f32[4,4,32,128]{3,2,1,0:T(8,128)}), f32[4,4,32,128]{3,2,1,0:T(8,128)S(1)}, u32[]{:S(2)}, u32[]{:S(2)}) async-start(f32[4,4,32,128]{3,2,1,0:T(8,128)} %bitcast.74), calls=%async_computation.1 | async-start | bytes 524288 | tf_op jit(solution)/shard_map/all_to_all | solution.py:200
  67.1 51.8 %all-gather.2.cloned.1.call-start = ((), (), s32[]{:S(2)}) async-start(), calls=%async_computation.3 | async-start | bytes 1310720 | tf_op jit(solution)/shard_map/all_gather | solution.py:185
  67.8 0.6 copy-start.7
  74.2 0.8 copy-start.4
  100.1 17.7 %all-to-all-start.2 = ((f32[4,256,256]{2,1,0:T(8,128)}), f32[4,256,256]{2,1,0:T(8,128)S(1)}, u32[]{:S(2)}, u32[]{:S(2)}) async-start(f32[4,256,256]{2,1,0:T(8,128)} %pad_maximum_fusion), calls=%async_computation.2 | async-start | bytes 2097152 | tf_op jit(solution)/shard_map/all_to_all | solution.py:251
Sparse Core Ops, SparseCore 0:
  69.7 28.3 all-gather.1

commit v4 on v3

--- a/solution.py
+++ b/solution.py
@@ -13,7 +13,7 @@
 SIGMA_TWO = 0.8
 CROSS_CORR = 0.5
 NUGGET = 0.1
-BLOCK = 32
+BLOCK = 16
 GROUP = 4
 LANES = 128
 TILE = 512

time: 132 us -> 130 us (0.985)
  Pallas kernels: 46.6 us -> 44.9 us
    pallas_call x2, Pallas kernels: 30.9 us -> 29.2 us  [factor(): pl.pallas_call(functools.partial(eliminate, steps), out_shape=(shape, sha...]
  transfers between devices with their start and end apart: 7 -> 7, of which waited for: 2 -> 2; matrix products, arithmetic and copies ran while one was open for 18% -> 19% of each run, Pallas kernels for 36% -> 35%
where the time goes in v4:
time: 130 us; the launch traced here: 129 us
  Pallas kernels  44.9 us (35%)
  waiting for transfers between devices  23.2 us (18%)
  local copies, waits for them, and re-layouts  14.8 us (11%)
  between operations  14.3 us (11%)
  starting transfers between devices  13.6 us (10%)
  matrix products  12.7 us (10%)
  other arithmetic  5.89 us (5%)
    pallas_call x2, Pallas kernels, factor(): pl.pallas_call(functools.partial(eliminate, steps), out_shape=(shape, sha...  29.2 us
    pallas_call x2, Pallas kernels, covariance(): pl.pallas_call(gather_covariance, grid=(count, points // tile), in_specs=...  15.7 us
    all_to_all x1, waiting for transfers between devices, per_device(): pack = lax.all_to_all(pack, 'gen', split_axis=0, concat_axis=0, tiled=True)  12.8 us
    all_to_all x1, waiting for transfers between devices, per_device(): lax.all_to_all(spread, 'gen', split_axis=1, concat_axis=4, tiled=True)  9.87 us
    all_to_all x1, starting transfers between devices, per_device(): lax.all_to_all(spread, 'gen', split_axis=1, concat_axis=4, tiled=True)  5.29 us
    all_to_all x1, starting transfers between devices, per_device(): pack = lax.all_to_all(pack, 'gen', split_axis=0, concat_axis=0, tiled=True)  4.14 us
    unnamed x22, local copies, waits for them, and re-layouts  3.74 us
    all_to_all x1, starting transfers between devices, per_device(): lax.all_to_all(leaf_pack, 'gen', split_axis=0, concat_axis=0, tiled=True)  3.41 us
  transfers between devices with their start and end apart: 7, of which 2 were waited for; matrix products, arithmetic and copies ran while one was open for 19% of the time, Pallas kernels for 35%

profile of v4, /device:TPU:0, one launch (start us, length us, event | category | flops | bytes accessed | tf_op | source)
XLA Modules:
  0.0 129.4 jit_solution(16217371724804137628)
XLA Ops:
  7.2 2.4 %copy.52 = bf16[2,4,2,2,128,128]{5,4,3,2,0,1:T(8,128)(2,1)} copy(bf16[2,4,2,2,128,128]{5,4,3,2,1,0:T(8,128)(2,1)} %bitcast.83) | data formatting | bytes 2097152 | tf_op jit(solution)/shard_map/reshape;squeeze | solution.py:170
  9.6 5.3 %all-to-all-start = ((bf16[2,4,2,2,128,128]{5,4,3,2,0,1:T(8,128)(2,1)}), bf16[2,4,2,2,128,128]{5,4,3,2,0,1:T(8,128)(2,1)S(1)}, u32[]{:S(2)}, u32[]{:S(2)}) async-start(bf16[2,4,2,2,128,128]{5,4,3,2,0,1:T(8,128)(2,1)} %copy.52), calls=%async_computation | async-start | bytes 2097152 | tf_op jit(solution)/shard_map/all_to_all | solution.py:171
  17.0 1.4 %copy.57.near_ref = f32[4,512,2]{2,1,0:T(8,128)} copy(f32[4,512,2]{1,2,0:T(2,128)S(1)} %bitcast.94) | data formatting | bytes 32768 | tf_op jit(solution)/shard_map/transpose | solution.py:137
  18.7 9.9 %all-to-all-done = bf16[2,4,2,2,128,128]{5,4,3,2,0,1:T(8,128)(2,1)S(1)} async-done(((bf16[2,4,2,2,128,128]{5,4,3,2,0,1:T(8,128)(2,1)}), bf16[2,4,2,2,128,128]{5,4,3,2,0,1:T(8,128)(2,1)S(1)}, u32[]{:S(2)}, u32[]{:S(2)}) %all-to-all-start) | async-done | bytes 1048608 | tf_op jit(solution)/shard_map/all_to_all | solution.py:171
  28.6 1.2 constant_dynamic-slice_fusion
  29.8 1.2 multiply_add_fusion
  31.1 14.8 %shard_map.84 = (f32[4,128,128]{2,1,0:T(8,128)}, f32[4,128,128]{2,1,0:T(8,128)}) custom-call(f32[4,128,128]{2,1,0:T(8,128)} %get-tuple-element.38.gram_ref), custom_call_target="tpu_custom_call" | custom-call | tf_op jit(solution)/shard_map/pallas_call | solution.py:76
  45.9 1.1 broadcast_multiply_fusion
  47.0 9.9 %shard_map.85 = f32[4,128,128]{2,1,0:T(8,128)} custom-call(f32[4,512,2]{2,1,0:T(8,128)} %copy.57.near_ref, f32[4,2,512]{2,1,0:T(2,128)} %bitcast.95, bf16[4,2,512,128]{3,2,1,0:T(8,128)(2,1)} %bitcast.78, bf16[4,2,512,128]{3,2,1,0:T(8,128)(2,1)} %bitcast.79), custom_call_target="tpu_custom_call" | custom-call | tf_op jit(solution)/shard_map/pallas_call | solution.py:126
  56.9 1.6 %fusion.16 = f32[4,128,128]{2,1,0:T(8,128)S(1)} fusion(f32[4,128,128]{2,1,0:T(8,128)S(1)} %broadcast_multiply_fusion, f32[4,128,128]{2,1,0:T(8,128)} %shard_map.85, f32[4,128,128]{2,1,0:T(8,128)S(1)} %get-tuple-element.39), kind=kOutput, calls=%fused_computation.26 | convolution fusion | flops 100794368 | bytes 1048576 | tf_op jit(solution)/shard_map/lab,lcb->lac/dot_general | solution.py:141
  62.7 3.4 %all-to-all-start.1 = ((f32[4,4,32,128]{3,2,1,0:T(8,128)}), f32[4,4,32,128]{3,2,1,0:T(8,128)S(1)}, u32[]{:S(2)}, u32[]{:S(2)}) async-start(f32[4,4,32,128]{3,2,1,0:T(8,128)} %bitcast.74), calls=%async_computation.1 | async-start | bytes 524288 | tf_op jit(solution)/shard_map/all_to_all | solution.py:200
  67.4 5.8 %shard_map.87 = f32[2,128,128]{2,1,0:T(8,128)} custom-call(f32[2,512,2]{2,1,0:T(8,128)} %copy.63.near_ref, f32[2,2,512]{2,1,0:T(2,128)} %copy-done.7, bf16[2,2,512,128]{3,2,1,0:T(8,128)(2,1)} %get-tuple-element.29.near_rows_ref, bf16[2,2,512,128]{3,2,1,0:T(8,128)(2,1)} %collective-permute-done.2.far_rows_ref), custom_call_target="tpu_custom_call" | custom-call | tf_op jit(solution)/shard_map/pallas_call | solution.py:126
  74.0 1.3 fusion.20
  76.7 1.9 %convolution_add_fusion.gram_ref = f32[2,256,256]{2,1,0:T(8,128)} fusion(f32[2,128,256]{2,1,0:T(8,128)S(1)} %get-tuple-element.31, f32[2,128,256]{2,1,0:T(8,128)S(1)} %get-tuple-element.30, f32[2,256]{1,0:T(2,128)S(1)} %broadcast_subtract_fusion, f32[256,256]{1,0:T(8,128)S(1)} %fusion.19, f32[2,256]{1,0:T(2,128)S(1)} %compare_convert_fusion), kind=kOutput, calls=%fused_computation.1 | convolution fusion | flops 403177472 | bytes 1314816 | tf_op jit(solution)/shard_map/lak,laj->lkj/dot_general | solution.py:225
  78.5 14.4 %shard_map.86 = (f32[2,256,256]{2,1,0:T(8,128)}, f32[2,256,256]{2,1,0:T(8,128)}) custom-call(f32[2,256,256]{2,1,0:T(8,128)} %convolution_add_fusion.gram_ref), custom_call_target="tpu_custom_call" | custom-call | tf_op jit(solution)/shard_map/pallas_call | solution.py:76
  92.9 1.7 %fusion.11 = f32[2,256,256]{2,1,0:T(8,128)S(1)} fusion(f32[2,256,256]{2,1,0:T(8,128)} %get-tuple-element.9, f32[2,128,256]{2,1,0:T(8,128)S(1)} %get-tuple-element.31, f32[2,128,256]{2,1,0:T(8,128)S(1)} %get-tuple-element.30, f32[2,256]{1,0:T(2,128)S(1)} %compare_convert_fusion), kind=kOutput, calls=%fused_computation.19 | convolution fusion | flops 402915328 | bytes 1574912 | tf_op jit(solution)/shard_map/lak,ljk->laj/dot_general | solution.py:228
  96.3 1.0 fusion.37
  97.4 1.0 pad_maximum_fusion
  98.5 4.1 %all-to-all-start.2 = ((f32[4,256,256]{2,1,0:T(8,128)}), f32[4,256,256]{2,1,0:T(8,128)S(1)}, u32[]{:S(2)}, u32[]{:S(2)}) async-start(f32[4,256,256]{2,1,0:T(8,128)} %pad_maximum_fusion), calls=%async_computation.2 | async-start | bytes 2097152 | tf_op jit(solution)/shard_map/all_to_all | solution.py:251
  103.3 12.8 %all-to-all-done.2 = f32[4,256,256]{2,1,0:T(8,128)S(1)} async-done(((f32[4,256,256]{2,1,0:T(8,128)}), f32[4,256,256]{2,1,0:T(8,128)S(1)}, u32[]{:S(2)}, u32[]{:S(2)}) %all-to-all-start.2) | async-done | bytes 1048608 | tf_op jit(solution)/shard_map/all_to_all | solution.py:251
  116.1 1.1 fusion.35
  117.2 1.3 %copy.55 = f32[2,4,2,128,128]{4,3,2,1,0:T(8,128)S(1)} copy(f32[2,4,2,128,128]{4,3,2,0,1:T(8,128)} %all-gather.2.cloned.1.call-done) | data formatting | bytes 2097152 | tf_op jit(solution)/shard_map/all_gather | solution.py:185
  118.5 2.2 %convolution_bitcast_fusion = f32[16,1,2,128,128]{3,4,2,0,1:T(8,128)S(1)} fusion(f32[16,128,128,1]{2,1,3,0:T(8,128)S(1)} %bitcast.84, bf16[16,1,2,128,128]{4,3,2,1,0:T(8,128)(2,1)} %param.6), kind=kOutput, calls=%fused_computation | convolution fusion | flops 805306368 | bytes 4194304 | tf_op jit(solution)/shard_map/lvnk,ljk->lvnj/dot_general | solution.py:194
  120.7 1.8 %copy.67 = f32[16,1,2,128,128]{4,3,2,1,0:T(8,128)} copy(f32[16,1,2,128,128]{3,4,2,0,1:T(8,128)S(1)} %convolution_bitcast_fusion) | data formatting | bytes 4194304
  (60 shorter events, 12.4 us)
Async XLA Ops:
  7.2 11.3 %copy-start = (bf16[16,1,128,256]{3,2,1,0:T(8,128)(2,1)S(1)}, bf16[16,1,128,256]{3,2,1,0:T(8,128)(2,1)}, u32[]{:S(2)}) copy-start(bf16[16,1,128,256]{3,2,1,0:T(8,128)(2,1)} %param.8) | copy-start | bytes 3145732
  7.2 9.0 %copy-start.8 = (s32[16,1]{0,1:T(1,128)S(1)}, s32[16,1]{0,1:T(1,128)}, u32[]{:S(2)}) copy-start(s32[16,1]{0,1:T(1,128)} %param.7) | copy-start | bytes 196
  9.6 8.8 %copy-start.9 = (s32[8,1]{0,1:T(1,128)S(1)}, s32[8,1]{0,1:T(1,128)}, u32[]{:S(2)}) copy-start(s32[8,1]{0,1:T(1,128)} %param.9) | copy-start | bytes 100
  9.6 18.9 %all-to-all-start = ((bf16[2,4,2,2,128,128]{5,4,3,2,0,1:T(8,128)(2,1)}), bf16[2,4,2,2,128,128]{5,4,3,2,0,1:T(8,128)(2,1)S(1)}, u32[]{:S(2)}, u32[]{:S(2)}) async-start(bf16[2,4,2,2,128,128]{5,4,3,2,0,1:T(8,128)(2,1)} %copy.52), calls=%async_computation | async-start | bytes 2097152 | tf_op jit(solution)/shard_map/all_to_all | solution.py:171
  15.6 14.2 %copy-start.5 = (f32[2,1,2,2,512]{4,3,2,1,0:T(2,128)}, f32[2,1,2,2,512]{4,3,2,1,0:T(2,128)S(1)}, u32[]{:S(2)}) copy-start(f32[2,1,2,2,512]{4,3,2,1,0:T(2,128)S(1)} %constant_dynamic-slice_fusion.5) | copy-start | bytes 49156
  15.6 51.2 %collective-permute-start.1 = (f32[2,2,512]{2,1,0:T(2,128)S(1)}, f32[2,2,512]{2,1,0:T(2,128)S(1)}, u32[]{:S(2)}, u32[]{:S(2)}) collective-permute-start(f32[2,2,512]{2,1,0:T(2,128)S(1)} %get-tuple-element.36), channel_id=1, source_target_pairs={{0,4},{4,0},{8,12},{12,8},{16,20},{20,16},{24,28},{28,24},{1,5},{5... | collective-permute-start | bytes 24584 | tf_op jit(solution)/shard_map/ppermute | solution.py:24
  28.6 2.5 %copy-start.1 = (bf16[2,1,2,2,4,128,128]{6,5,4,3,2,0,1:T(8,128)(2,1)}, bf16[2,1,2,2,4,128,128]{6,5,4,3,2,0,1:T(8,128)(2,1)S(1)}, u32[]{:S(2)}) copy-start(bf16[2,1,2,2,4,128,128]{6,5,4,3,2,0,1:T(8,128)(2,1)S(1)} %copy.53) | copy-start | bytes 3145732
  47.0 12.4 %copy-start.2 = (f32[4,128,128]{2,1,0:T(8,128)}, f32[4,128,128]{2,1,0:T(8,128)S(1)}, u32[]{:S(2)}) copy-start(f32[4,128,128]{2,1,0:T(8,128)S(1)} %broadcast_multiply_fusion) | copy-start | bytes 786436
  47.0 12.0 %copy-start.6 = (f32[4,128,128]{2,1,0:T(8,128)S(1)}, f32[4,128,128]{2,1,0:T(8,128)}, u32[]{:S(2)}) copy-start(f32[4,128,128]{2,1,0:T(8,128)} %get-tuple-element.8) | copy-start | bytes 786436
  60.2 13.0 %collective-permute-start = (f32[2,128,512]{2,1,0:T(8,128)}, f32[2,128,512]{2,1,0:T(8,128)S(1)}, u32[]{:S(2)}, u32[]{:S(2)}) collective-permute-start(f32[2,128,512]{2,1,0:T(8,128)} %fusion.2), channel_id=1, source_target_pairs={{0,4},{4,0},{8,12},{12,8},{16,20},{20,16},{24,28},{28,24},{1,5},{5... | collective-permute-start | bytes 1572872 | tf_op jit(solution)/shard_map/ppermute | solution.py:24
  60.2 6.6 %collective-permute-start.2 = (bf16[2,2,512,128]{3,2,1,0:T(8,128)(2,1)}, bf16[2,2,512,128]{3,2,1,0:T(8,128)(2,1)}, u32[]{:S(2)}, u32[]{:S(2)}) collective-permute-start(bf16[2,2,512,128]{3,2,1,0:T(8,128)(2,1)} %get-tuple-element.28), channel_id=1, source_target_pairs={{0,4},{4,0},{8,12},{12,8},{16,20},{20,16},{24,28},{28,24},{1,5},{5... | collective-permute-start | bytes 1572872 | tf_op jit(solution)/shard_map/ppermute | solution.py:24
  60.9 14.4 %copy-start.3 = (f32[4,128,128]{2,1,0:T(8,128)S(1)}, f32[4,128,128]{2,1,0:T(8,128)}, u32[]{:S(2)}) copy-start(f32[4,128,128]{2,1,0:T(8,128)} %copy-done.2) | copy-start | bytes 786436
  62.7 35.8 %all-to-all-start.1 = ((f32[4,4,32,128]{3,2,1,0:T(8,128)}), f32[4,4,32,128]{3,2,1,0:T(8,128)S(1)}, u32[]{:S(2)}, u32[]{:S(2)}) async-start(f32[4,4,32,128]{3,2,1,0:T(8,128)} %bitcast.74), calls=%async_computation.1 | async-start | bytes 524288 | tf_op jit(solution)/shard_map/all_to_all | solution.py:200
  66.1 51.2 %all-gather.2.cloned.1.call-start = ((), (), s32[]{:S(2)}) async-start(), calls=%async_computation.3 | async-start | bytes 1310720 | tf_op jit(solution)/shard_map/all_gather | solution.py:185
  66.8 0.6 copy-start.7
  73.2 0.8 copy-start.4
  98.5 17.7 %all-to-all-start.2 = ((f32[4,256,256]{2,1,0:T(8,128)}), f32[4,256,256]{2,1,0:T(8,128)S(1)}, u32[]{:S(2)}, u32[]{:S(2)}) async-start(f32[4,256,256]{2,1,0:T(8,128)} %pad_maximum_fusion), calls=%async_computation.2 | async-start | bytes 2097152 | tf_op jit(solution)/shard_map/all_to_all | solution.py:251
Sparse Core Ops, SparseCore 0:
  68.7 28.3 all-gather.1
